TPU v7x, 32 devices: a whole 2x2x4 slice. The times are simulated.
32 devices in a mesh: groups: 2 (over y), job: 4 (over x, core), tensor: 4 (over z).
Axes of the slice: x: 2, y: 2, z: 4, core: 2. Of those that a mesh axis runs over, the one named last changes fastest.
Arguments:
- tokens: bfloat16 [12288, 8192], P(('groups', 'job'), 'tensor'), parts along dimension 0, may hold values from -6 to 6
- frozen_key_weight: bfloat16 [8192, 1024], P('tensor'), may hold values from -0.0625 to 0.0625
- adapter_down_maps: bfloat16 [32, 8192, 64], P('job', 'tensor'), may hold values from -0.0625 to 0.0625
- adapter_up_maps: bfloat16 [32, 64, 1024], P('job', 'tensor'), may hold values from -0.75 to 0.75
- cotangent: bfloat16 [12288, 1024], P(('groups', 'job', 'tensor')), parts along dimension 0, may hold values from -6 to 6
- block_owner_job: int32 [96, 1], P('groups'), parts along dimension 0, may hold values from 0 to 3; in each aligned block of 12 rows (0 to 11, 12 to 23, ...) at most 4 rows name the same one
- block_local_adapter: int32 [96], P('groups'), parts along dimension 0, may hold values from 0 to 7
- block_live_rows: int32 [96], P('groups'), parts along dimension 0, may hold values from 0 to 128
Outputs:
- projected: bfloat16 [12288, 1024], P(('groups', 'job', 'tensor')), parts along dimension 0
- grad_tokens: bfloat16 [12288, 8192], P(('groups', 'job'), 'tensor'), parts along dimension 0
- grad_down: float32 [64, 8192, 64], P(('groups', 'job'), 'tensor'), parts along dimension 0
- grad_up: float32 [64, 64, 1024], P(('groups', 'job'), 'tensor'), parts along dimension 0
There are 2 independent parts, one for each index of `groups`. A program takes and returns all parts, laid end to end along the dimension named above; an argument that names none is the same for every part. Nothing has to cross between parts.
Inputs may be any that keep to these rules, and one draw needn't show every extreme that they name: `block_owner_job`: in each aligned run of 12 blocks (the slots of one index of job), at most 4 blocks name the same owner.
All inputs are finite; a program needn't handle non-finite values.
Results may differ from a plain program's by a relative error of at most 0.015.
Values may be sent and summed in bfloat16 or wider, within the bound.
A program may use at most 128 MiB of HBM per device.

v0:
```python
import jax
import jax.numpy as jnp
from jax import lax
from jax.sharding import PartitionSpec as P

BLOCK = 128


adapter_scale = 2.0


def local(
    tokens,
    frozen_key_weight,
    adapter_down_maps,
    adapter_up_maps,
    cotangent,
    block_owner_job,
    block_local_adapter,
    block_live_rows,
):
    job_count = lax.axis_size("job")
    own_job = lax.axis_index("job")
    row_total = tokens.shape[0]
    block_count = row_total // BLOCK
    local_adapters = adapter_down_maps.shape[0]
    width_portion = adapter_down_maps.shape[1]
    full_rank_values = adapter_down_maps.shape[2]
    rank_portion = adapter_up_maps.shape[1]
    output_width = adapter_up_maps.shape[2]
    owners_all = block_owner_job[:, 0].reshape(job_count, block_count)
    locals_all = block_local_adapter.reshape(job_count, block_count)
    fills_all = block_live_rows.reshape(job_count, block_count)
    my_owner = lax.dynamic_index_in_dim(owners_all, own_job, 0, keepdims=False)
    my_local = lax.dynamic_index_in_dim(locals_all, own_job, 0, keepdims=False)
    my_fill = lax.dynamic_index_in_dim(fills_all, own_job, 0, keepdims=False)
    adapter_ids = my_owner * local_adapters + my_local
    live_rows = (jnp.arange(BLOCK, dtype=jnp.int32)[None, :] < my_fill[:, None]).reshape(row_total)
    masked = tokens * live_rows[:, None].astype(jnp.bfloat16)
    row_blocks = masked.reshape(block_count, BLOCK, width_portion)
    every_down, every_up = (
        lax.all_gather(adapter_down_maps, "job", axis=0, tiled=True),
        lax.all_gather(adapter_up_maps, "job", axis=0, tiled=True),
    )
    block_down_maps = jnp.take(every_down, adapter_ids, axis=0)
    up_blocks = jnp.take(every_up, adapter_ids, axis=0)
    rank_terms = jnp.einsum(
        "bnd,bdr->bnr", row_blocks, block_down_maps, preferred_element_type=jnp.float32
    ).reshape(row_total, full_rank_values)
    rank_mine = lax.psum_scatter(
        rank_terms.astype(jnp.bfloat16), "tensor", scatter_dimension=1, tiled=True
    ).astype(jnp.float32)
    rank_blocks = rank_mine.reshape(block_count, BLOCK, rank_portion)
    adapter_rows = jnp.einsum(
        "seu,sui->sei", rank_blocks, up_blocks.astype(jnp.float32), precision=lax.Precision.HIGHEST
    ).reshape(row_total, output_width)
    projected = lax.psum_scatter(
        (
            jnp.dot(masked, frozen_key_weight, preferred_element_type=jnp.float32)
            + adapter_scale * adapter_rows
        ).astype(jnp.bfloat16),
        "tensor",
        scatter_dimension=0,
        tiled=True,
    )
    grad_full = lax.all_gather(cotangent, "tensor", axis=0, tiled=True)
    grad_blocks = grad_full.reshape(block_count, BLOCK, output_width)
    rank_grad_mine = (
        adapter_scale
        * jnp.einsum("ald,afd->alf", grad_blocks, up_blocks, preferred_element_type=jnp.float32)
    ).astype(jnp.bfloat16)
    rank_grad_all = lax.all_gather(
        rank_grad_mine.reshape(row_total, rank_portion), "tensor", axis=1, tiled=True
    )
    rank_grad_blocks = rank_grad_all.reshape(block_count, BLOCK, full_rank_values)
    grad_rows = lax.dot_general(
        grad_full, frozen_key_weight, (((1,), (1,)), ((), ())), preferred_element_type=jnp.float32
    )
    grad_rows = grad_rows + jnp.einsum(
        "bnr,bdr->bnd", rank_grad_blocks, block_down_maps, preferred_element_type=jnp.float32
    ).reshape(row_total, width_portion)
    grad_tokens = (grad_rows * live_rows[:, None].astype(jnp.float32)).astype(jnp.bfloat16)
    down_terms = jnp.einsum(
        "bnd,bnr->bdr", row_blocks, rank_grad_blocks, preferred_element_type=jnp.float32
    ).reshape(block_count, -1)
    up_map_terms = (
        adapter_scale
        * jnp.einsum(
            "xhw,xhk->xwk",
            rank_blocks,
            grad_blocks.astype(jnp.float32),
            precision=lax.Precision.HIGHEST,
        )
    ).reshape(block_count, -1)
    adapter_range = jnp.arange(job_count * local_adapters, dtype=jnp.int32)
    onehot = (adapter_ids[None, :] == adapter_range[:, None]).astype(jnp.float32)
    dense_down = jnp.einsum(
        "ab,bx->ax", onehot, down_terms, precision=lax.Precision.HIGHEST
    ).reshape(job_count, local_adapters, -1)
    dense_up = jnp.einsum(
        "ab,bx->ax", onehot, up_map_terms, precision=lax.Precision.HIGHEST
    ).reshape(job_count, local_adapters, -1)
    got_down, got_up = (
        lax.all_to_all(
            dense_down.astype(jnp.bfloat16), "job", split_axis=0, concat_axis=0, tiled=True
        ).astype(dense_down.dtype),
        lax.all_to_all(
            dense_up.astype(jnp.bfloat16), "job", split_axis=0, concat_axis=0, tiled=True
        ).astype(dense_up.dtype),
    )
    grad_down = jnp.sum(got_down, axis=0)
    grad_up = jnp.sum(got_up, axis=0)
    grad_down = grad_down.reshape(local_adapters, width_portion, full_rank_values)
    grad_up = grad_up.reshape(local_adapters, rank_portion, output_width)
    return (projected, grad_tokens, grad_down, grad_up)


def solution(mesh):
    placed = (
        P(("groups", "job"), "tensor"),
        P("tensor", None),
        P("job", "tensor", None),
        P("job", "tensor", None),
        P(("groups", "job", "tensor"), None),
        P("groups", None),
        P("groups"),
        P("groups"),
    )
    return jax.shard_map(
        local,
        mesh=mesh,
        in_specs=placed,
        out_specs=(
            P(("groups", "job", "tensor"), None),
            P(("groups", "job"), "tensor"),
            P(("groups", "job"), "tensor", None),
            P(("groups", "job"), "tensor", None),
        ),
        check_vma=False,
    )
```

profile of v0, /device:TPU:0, one launch (start us, length us, event | category | flops | bytes accessed | tf_op | source)
XLA Modules:
  0.0 309.0 jit_solution(3103329718001396584)
XLA Ops:
  9.9 1.3 reduce.3
  11.3 0.7 reshape.157
  12.0 0.7 reshape.155
  13.5 6.0 %broadcast_multiply_fusion.1 = bf16[1536,2048]{1,0:T(8,128)(2,1)} fusion(bf16[1536,2048]{1,0:T(8,128)(2,1)} %param.8, bf16[1536]{0:T(1024)(128)(2,1)S(1)} %get-tuple-element.15), kind=kLoop, calls=%fused_computation.11 | loop fusion | flops 3145728 | bytes 12585984 | tf_op jit(solution)/shard_map/mul | solution.py:39
  19.5 9.5 %all-gather.6.cloned.1.call-done = bf16[32,16,1024]{2,1,0:T(8,128)(2,1)} async-done(((bf16[8,16,1024]{2,1,0:T(8,128)(2,1)}), bf16[32,16,1024]{2,1,0:T(8,128)(2,1)}) %all-gather.6.cloned.1.call-update) | async-done | bytes 1048592 | tf_op jit(solution)/shard_map/all_gather | solution.py:43
  29.0 1.8 gather_fusion.1
  30.8 63.3 %all-gather.8.cloned.1.call-done = bf16[1536,1024]{1,0:T(8,128)(2,1)} async-done(((bf16[384,1024]{1,0:T(8,128)(2,1)}), bf16[1536,1024]{1,0:T(8,128)(2,1)}) %all-gather.8.cloned.1.call-update) | async-done | bytes 3145744 | tf_op jit(solution)/shard_map/all_gather | solution.py:66
  94.1 2.9 fusion.8
  97.0 13.9 %all_gather.15 = bf16[1536,64]{0,1:T(8,128)(2,1)S(1)} all-gather(bf16[1536,16]{0,1:T(8,128)(2,1)S(1)} %bitcast.81), channel_id=1, replica_groups=mesh['groups'=2,'job'=4,'tensor'=4] {'tensor'}, dimensions={1}, use_global_device_ids=true | all-gather | bytes 245760 | tf_op jit(solution)/shard_map/all_gather | solution.py:72
  111.6 9.4 %fusion.9 = f32[12,2048,64]{2,1,0:T(8,128)} fusion(bf16[12,128,2048]{2,1,0:T(8,128)(2,1)} %bitcast.74, bf16[1536,64]{0,1:T(8,128)(2,1)S(1)} %all_gather.15), kind=kOutput, calls=%fused_computation.25 | convolution fusion | flops 402653184 | bytes 12779520 | tf_op jit(solution)/shard_map/bnd,bnr->bdr/dot_general | solution.py:83
  120.9 14.3 %reshape.185 = f32[12,131072,1]{1,0,2:T(8,128)} reshape(f32[12,2048,64]{2,1,0:T(8,128)} %fusion.9) | data formatting | bytes 12582912 | tf_op jit(solution)/shard_map/reshape | solution.py:85
  135.3 11.0 %convolution_convert_fusion = bf16[4,8,131072]{2,1,0:T(8,128)(2,1)} fusion(f32[12,131072,1]{1,0,2:T(8,128)} %reshape.185, s32[4,8]{1,0:T(4,128)S(1)} %multiply_add_fusion, s32[12]{0:T(128)S(1)} %bitcast.82), kind=kOutput, calls=%fused_computation.2 | convolution fusion | flops 608174464 | bytes 14680240 | tf_op jit(solution)/shard_map/ab,bx->ax/dot_general | solution.py:97
  146.3 5.6 %all-to-all-start = ((bf16[4,8,131072]{2,1,0:T(8,128)(2,1)}), bf16[4,8,131072]{2,1,0:T(8,128)(2,1)}, u32[]{:S(2)}, u32[]{:S(2)}) async-start(bf16[4,8,131072]{2,1,0:T(8,128)(2,1)} %convolution_convert_fusion), calls=%async_computation.2 | async-start | bytes 16777216 | tf_op jit(solution)/shard_map/all_to_all | solution.py:104
  152.7 4.1 %gather_fusion = bf16[12,2048,64]{1,2,0:T(8,128)(2,1)S(1)} fusion(bf16[32,2048,64]{1,2,0:T(8,128)(2,1)} %all-gather.4.cloned.1.call-done, s32[1024]{0:T(1024)S(1)} %pad_clamp_fusion), kind=kCustom, calls=%fused_computation | custom fusion | bytes 6291504 | tf_op jit(solution)/shard_map/jit(_take)/gather | solution.py:45
  156.8 5.1 %fusion.6 = bf16[12,8,8,128]{3,2,1,0:T(8,128)(2,1)S(1)} fusion(bf16[12,128,2048]{2,1,0:T(8,128)(2,1)} %bitcast.75, bf16[12,2048,64]{1,2,0:T(8,128)(2,1)S(1)} %gather_fusion, pred[12]{0:T(512)(128)(4,1)S(1)} %get-tuple-element.12), kind=kOutput, calls=%fused_computation.18 | convolution fusion | flops 404324352 | bytes 9633804 | tf_op jit(solution)/shard_map/bnd,bdr->bnr/dot_general | solution.py:47
  161.9 0.7 copy.54
  162.7 21.9 %reduce-scatter.3.cloned.1.call-done = bf16[1536,16]{0,1:T(8,128)(2,1)} async-done(((bf16[1536,64]{0,1:T(8,128)(2,1)}), bf16[1536,16]{0,1:T(8,128)(2,1)}) %reduce-scatter.3.cloned.1.call-update) | async-done | bytes 49168 | tf_op jit(solution)/shard_map/reduce_scatter | solution.py:50
  184.6 2.0 broadcast_multiply_fusion
  186.8 10.0 %fusion.2 = bf16[1536,1024]{1,0:T(8,128)(2,1)} fusion(f32[12,128,1024]{2,1,0:T(8,128)S(1)} %broadcast_multiply_fusion, bf16[1536,2048]{1,0:T(8,128)(2,1)} %broadcast_multiply_fusion.1, bf16[2048,1024]{1,0:T(8,128)(2,1)S(1)} %copy-done.6), kind=kOutput, calls=%fused_computation.9 | convolution fusion | flops 6445596672 | bytes 19922944 | tf_op jit(solution)/shard_map/dot_general | solution.py:59
  196.8 48.3 %all-to-all-done = bf16[4,8,131072]{2,1,0:T(8,128)(2,1)} async-done(((bf16[4,8,131072]{2,1,0:T(8,128)(2,1)}), bf16[4,8,131072]{2,1,0:T(8,128)(2,1)}, u32[]{:S(2)}, u32[]{:S(2)}) %all-to-all-start) | async-done | bytes 8388640 | tf_op jit(solution)/shard_map/all_to_all | solution.py:104
  245.1 7.1 %convert_reduce_fusion = f32[8,131072]{1,0:T(8,128)} fusion(bf16[4,8,131072]{2,1,0:T(8,128)(2,1)} %all-to-all-done), kind=kLoop, calls=%fused_computation.4 | loop fusion | flops 7340032 | bytes 12582912 | tf_op jit(solution)/shard_map/reduce_sum | solution.py:111
  252.2 8.7 %reshape.164 = f32[8,2048,64]{2,1,0:T(8,128)} reshape(f32[8,131072]{1,0:T(8,128)} %convert_reduce_fusion) | data formatting | bytes 8388608 | tf_op jit(solution)/shard_map/reshape | solution.py:113
  260.9 6.8 %copy.27 = f32[8,2048,64]{1,2,0:T(8,128)} copy(f32[8,2048,64]{2,1,0:T(8,128)} %reshape.164) | data formatting | bytes 8388608
  267.7 6.4 %fusion.3 = f32[12,128,2048]{2,1,0:T(8,128)} fusion(bf16[12,2048,64]{1,2,0:T(8,128)(2,1)S(1)} %gather_fusion, pred[12]{0:T(512)(128)(4,1)S(1)} %get-tuple-element.12, bf16[1536,64]{0,1:T(8,128)(2,1)S(1)} %copy-done.3), kind=kOutput, calls=%fused_computation.15 | convolution fusion | flops 404226048 | bytes 15925260 | tf_op jit(solution)/shard_map/bnr,bdr->bnd/dot_general | solution.py:79
  274.1 1.5 convolution_multiply_fusion
  275.5 2.4 reshape.186
  277.9 3.2 %convolution_convert_fusion.1 = bf16[4,8,16384]{2,1,0:T(8,128)(2,1)} fusion(f32[12,16384,1]{1,0,2:T(8,128)} %reshape.186, s32[4,8]{1,0:T(4,128)S(1)} %multiply_add_fusion, s32[12]{0:T(128)S(1)} %bitcast.83), kind=kOutput, calls=%fused_computation.3 | convolution fusion | flops 76022144 | bytes 1835184 | tf_op jit(solution)/shard_map/ab,bx->ax/dot_general | solution.py:100
  281.1 4.5 %all-to-all-start.1 = ((bf16[4,8,16384]{2,1,0:T(8,128)(2,1)}), bf16[4,8,16384]{2,1,0:T(8,128)(2,1)}, u32[]{:S(2)}, u32[]{:S(2)}) async-start(bf16[4,8,16384]{2,1,0:T(8,128)(2,1)} %convolution_convert_fusion.1), calls=%async_computation.3 | async-start | bytes 2097152 | tf_op jit(solution)/shard_map/all_to_all | solution.py:107
  285.6 12.6 %fusion.1 = bf16[1536,2048]{1,0:T(8,128)(2,1)} fusion(f32[12,128,2048]{2,1,0:T(8,128)} %fusion.3, bf16[1536,1024]{1,0:T(8,128)(2,1)S(1)} %copy-done.1, bf16[2048,1024]{1,0:T(8,128)(2,1)} %param.9, f32[1536]{0:T(1024)S(1)} %copy-done.5), kind=kOutput, calls=%fused_computation.7 | convolution fusion | flops 6451888128 | bytes 26220544 | tf_op jit(solution)/shard_map/dot_general | solution.py:76
  298.2 1.7 all-to-all-done.1
  299.9 1.4 convert_reduce_fusion.1
  301.3 1.1 copy.53
  (35 shorter events, 5.2 us)
Async XLA Ops:
  7.2 21.9 %all-gather.6.cloned.1.call-start = ((), (), s32[]{:S(2)}) async-start(), calls=%async_computation.6 | async-start | bytes 1310720 | tf_op jit(solution)/shard_map/all_gather | solution.py:43
  7.9 86.2 %all-gather.8.cloned.1.call-start = ((), (), s32[]{:S(2)}) async-start(), calls=%async_computation.8 | async-start | bytes 3932160 | tf_op jit(solution)/shard_map/all_gather | solution.py:66
  8.6 144.0 %all-gather.4.cloned.1.call-start = ((), (), s32[]{:S(2)}) async-start(), calls=%async_computation.4 | async-start | bytes 10485760 | tf_op jit(solution)/shard_map/all_gather | solution.py:42
  110.9 0.7 copy-start.2
  146.3 98.8 %all-to-all-start = ((bf16[4,8,131072]{2,1,0:T(8,128)(2,1)}), bf16[4,8,131072]{2,1,0:T(8,128)(2,1)}, u32[]{:S(2)}, u32[]{:S(2)}) async-start(bf16[4,8,131072]{2,1,0:T(8,128)(2,1)} %convolution_convert_fusion), calls=%async_computation.2 | async-start | bytes 16777216 | tf_op jit(solution)/shard_map/all_to_all | solution.py:104
  151.9 32.7 %reduce-scatter.3.cloned.1.call-start = ((), (), s32[]{:S(2)}) async-start(), calls=%async_computation.5 | async-start | bytes 245760 | tf_op jit(solution)/shard_map/reduce_scatter | solution.py:50
  162.6 139.8 %reduce-scatter.5.cloned.1.call-start = ((), (), s32[]{:S(2)}) async-start(), calls=%async_computation.7 | async-start | bytes 3932160 | tf_op jit(solution)/shard_map/reduce_scatter | solution.py:57
  184.6 2.2 copy-start.6
  260.9 6.8 %copy-start.3 = (bf16[1536,64]{0,1:T(8,128)(2,1)S(1)}, bf16[1536,64]{0,1:T(8,128)(2,1)}, u32[]{:S(2)}) copy-start(bf16[1536,64]{0,1:T(8,128)(2,1)} %copy-done.2) | copy-start | bytes 589828
  267.7 6.4 %copy-start = (bf16[1536,1024]{1,0:T(8,128)(2,1)S(1)}, bf16[1536,1024]{1,0:T(8,128)(2,1)}, u32[]{:S(2)}) copy-start(bf16[1536,1024]{1,0:T(8,128)(2,1)} %all-gather.8.cloned.1.call-done) | copy-start | bytes 9437188
  267.7 6.4 %copy-start.4 = (bf16[1536,16]{0,1:T(8,128)(2,1)S(1)}, bf16[1536,16]{0,1:T(8,128)(2,1)}, u32[]{:S(2)}) copy-start(bf16[1536,16]{0,1:T(8,128)(2,1)} %reduce-scatter.3.cloned.1.call-done) | copy-start | bytes 147460
  274.1 11.5 %copy-start.1 = (bf16[1536,1024]{1,0:T(8,128)(2,1)S(1)}, bf16[1536,1024]{1,0:T(8,128)(2,1)}, u32[]{:S(2)}) copy-start(bf16[1536,1024]{1,0:T(8,128)(2,1)} %all-gather.8.cloned.1.call-done) | copy-start | bytes 9437188
  274.1 11.5 %copy-start.5 = (f32[1536]{0:T(1024)S(1)}, f32[1536]{0:T(1024)}, u32[]{:S(2)}) copy-start(f32[1536]{0:T(1024)} %get-tuple-element.14) | copy-start | bytes 18436
  281.1 18.8 %all-to-all-start.1 = ((bf16[4,8,16384]{2,1,0:T(8,128)(2,1)}), bf16[4,8,16384]{2,1,0:T(8,128)(2,1)}, u32[]{:S(2)}, u32[]{:S(2)}) async-start(bf16[4,8,16384]{2,1,0:T(8,128)(2,1)} %convolution_convert_fusion.1), calls=%async_computation.3 | async-start | bytes 2097152 | tf_op jit(solution)/shard_map/all_to_all | solution.py:107
Sparse Core Ops, SparseCore 0:
  9.6 19.4 all-gather.5
  30.6 63.4 all-gather.7
  95.7 56.9 all-gather.3
  162.8 21.7 reduce-scatter.2
  196.9 58.4 reduce-scatter.4
where the time goes:
time: 310 us; the launch traced here: 309 us
  waiting for transfers between devices  147 us (47%)
  matrix products  64 us (21%)
  local copies, waits for them, and re-layouts  42.9 us (14%)
  other arithmetic  16.5 us (5%)
  blocking collectives  13.9 us (4%)
  between operations  13.9 us (4%)
  starting transfers between devices  10.3 us (3%)
    all_gather x1, waiting for transfers between devices, local(): grad_full = lax.all_gather(cotangent, 'tensor', axis=0, tiled=True)  63.3 us
    all_to_all x1, waiting for transfers between devices, local(): lax.all_to_all(dense_down.astype(jnp.bfloat16), 'job', split_axis=0, conc...  48.3 us
    reduce_scatter x1, waiting for transfers between devices, local(): lax.psum_scatter(rank_terms.astype(jnp.bfloat16), 'tensor', scatter_dimen...  21.9 us
    reshape x1, local copies, waits for them, and re-layouts, local(): down_terms = jnp.einsum('bnd,bnr->bdr', row_blocks, rank_grad_blocks, pre...  14.3 us
    all_gather x1, blocking collectives, local(): lax.all_gather(rank_grad_mine.reshape(row_total, rank_portion), 'tensor',...  13.9 us
    dot_general x1, matrix products, local(): lax.dot_general(grad_full, frozen_key_weight, (((1,), (1,)), ((), ())), p...  12.6 us
    dot_general x1, matrix products, local(): jnp.einsum('ab,bx->ax', onehot, down_terms, precision=lax.Precision.HIGHEST)  11 us
    dot_general x1, matrix products, local(): jnp.dot(masked, frozen_key_weight, preferred_element_type=jnp.float32)  9.98 us
  transfers between devices with their start and end apart: 7, of which 6 were waited for; matrix products, arithmetic and copies ran while one was open for 40% of the time, Pallas kernels for 0%

commit v1 on v0

--- a/solution.py
+++ b/solution.py
@@ -1,15 +1,28 @@
+import functools
+
 import jax
 import jax.numpy as jnp
 from jax import lax
+from jax.experimental import pallas as pl
+from jax.experimental.pallas import tpu as pltpu
 from jax.sharding import PartitionSpec as P
 
 BLOCK = 128
+SLOT_CAP = 4
+VMEM_LIMIT = 48 * 1024 * 1024
 
 
 adapter_scale = 2.0
 
-
-def local(
+NT = (((1,), (1,)), ((), ()))
+TN = (((0,), (0,)), ((), ()))
+
+
+def dot(a, b, dims):
+    return lax.dot_general(a, b, dims, preferred_element_type=jnp.float32)
+
+
+def general(
     tokens,
     frozen_key_weight,
     adapter_down_maps,
@@ -115,6 +128,310 @@
     return (projected, grad_tokens, grad_down, grad_up)
 
 
+def rank_kernel(slot_ref, tokens_ref, down_ref, live_ref, out_ref):
+    block_rank = dot(down_ref[0], tokens_ref[...], NT)
+    out_ref[0] = (block_rank * live_ref[0]).astype(out_ref.dtype)
+
+
+def rank_partials(tokens, got_down, my_slot, live):
+    row_total, width = tokens.shape
+    block_count = row_total // BLOCK
+    rank = got_down.shape[1]
+    return pl.pallas_call(
+        rank_kernel,
+        grid_spec=pltpu.PrefetchScalarGridSpec(
+            num_scalar_prefetch=1,
+            grid=(block_count,),
+            in_specs=[
+                pl.BlockSpec((BLOCK, width), lambda b, slot: (b, 0)),
+                pl.BlockSpec((1, rank, width), lambda b, slot: (slot[b], 0, 0)),
+                pl.BlockSpec((1, 1, BLOCK), lambda b, slot: (b, 0, 0)),
+            ],
+            out_specs=pl.BlockSpec((1, rank, BLOCK), lambda b, slot: (b, 0, 0)),
+        ),
+        out_shape=jax.ShapeDtypeStruct((block_count, rank, BLOCK), jnp.bfloat16),
+        compiler_params=pltpu.CompilerParams(vmem_limit_bytes=VMEM_LIMIT),
+        cost_estimate=pl.CostEstimate(
+            flops=2 * row_total * width * rank,
+            bytes_accessed=2 * (row_total * width + block_count * rank * width),
+            transcendentals=0,
+        ),
+        name="rank_partials",
+    )(my_slot, tokens, got_down, live)
+
+
+def grad_tokens_kernel(per_step, slot_ref, cot_ref, weight_ref, rank_grad_ref, live_ref, *rest):
+    down_refs, out_ref = rest[:per_step], rest[per_step]
+    for k in range(per_step):
+        rows = pl.ds(k * BLOCK, BLOCK)
+        total = dot(cot_ref[rows, :], weight_ref[...], NT)
+        total = total + dot(rank_grad_ref[k], down_refs[k][0], TN)
+        out_ref[rows, :] = (total * live_ref[rows, :]).astype(out_ref.dtype)
+
+
+def token_grads(cot_full, weight, rank_grad, live_rows, got_down, my_slot, per_step):
+    row_total, key_width = cot_full.shape
+    width = weight.shape[0]
+    rank = got_down.shape[1]
+    step_rows = per_step * BLOCK
+    return pl.pallas_call(
+        functools.partial(grad_tokens_kernel, per_step),
+        grid_spec=pltpu.PrefetchScalarGridSpec(
+            num_scalar_prefetch=1,
+            grid=(row_total // step_rows,),
+            in_specs=[
+                pl.BlockSpec((step_rows, key_width), lambda i, slot: (i, 0)),
+                pl.BlockSpec((width, key_width), lambda i, slot: (0, 0)),
+                pl.BlockSpec((per_step, rank, BLOCK), lambda i, slot: (i, 0, 0)),
+                pl.BlockSpec((step_rows, 1), lambda i, slot: (i, 0)),
+            ]
+            + [
+                pl.BlockSpec(
+                    (1, rank, width),
+                    functools.partial(lambda k, i, slot: (slot[i * per_step + k], 0, 0), k),
+                )
+                for k in range(per_step)
+            ],
+            out_specs=pl.BlockSpec((step_rows, width), lambda i, slot: (i, 0)),
+        ),
+        out_shape=jax.ShapeDtypeStruct((row_total, width), jnp.bfloat16),
+        compiler_params=pltpu.CompilerParams(vmem_limit_bytes=VMEM_LIMIT),
+        cost_estimate=pl.CostEstimate(
+            flops=2 * row_total * width * (key_width + rank),
+            bytes_accessed=2 * (row_total * (width + key_width) + width * key_width),
+            transcendentals=0,
+        ),
+        name="token_grads",
+    )(my_slot, cot_full, weight, rank_grad, live_rows, *([got_down] * per_step))
+
+
+def down_terms_kernel(block_ref, valid_ref, tokens_ref, rank_grad_ref, out_ref):
+    step = pl.program_id(0)
+
+    @pl.when(valid_ref[step] > 0)
+    def _():
+        out_ref[0] = dot(rank_grad_ref[0], tokens_ref[...], (((1,), (0,)), ((), ()))).astype(
+            out_ref.dtype
+        )
+
+    @pl.when(valid_ref[step] == 0)
+    def _():
+        out_ref[...] = jnp.zeros_like(out_ref)
+
+
+def down_terms(tokens, rank_grad_live, slot_block, slot_valid):
+    width = tokens.shape[1]
+    slots = slot_block.shape[0]
+    rank = rank_grad_live.shape[1]
+    return pl.pallas_call(
+        down_terms_kernel,
+        grid_spec=pltpu.PrefetchScalarGridSpec(
+            num_scalar_prefetch=2,
+            grid=(slots,),
+            in_specs=[
+                pl.BlockSpec((BLOCK, width), lambda s, block, valid: (block[s], 0)),
+                pl.BlockSpec((1, rank, BLOCK), lambda s, block, valid: (block[s], 0, 0)),
+            ],
+            out_specs=pl.BlockSpec((1, rank, width), lambda s, block, valid: (s, 0, 0)),
+        ),
+        out_shape=jax.ShapeDtypeStruct((slots, rank, width), jnp.bfloat16),
+        compiler_params=pltpu.CompilerParams(vmem_limit_bytes=VMEM_LIMIT),
+        cost_estimate=pl.CostEstimate(
+            flops=2 * slots * BLOCK * width * rank,
+            bytes_accessed=2 * slots * (BLOCK * width + rank * width),
+            transcendentals=0,
+        ),
+        name="down_terms",
+    )(slot_block, slot_valid, tokens, rank_grad_live)
+
+
+def owner_sum_kernel(adapter_ref, valid_ref, got_ref, out_ref):
+    out_ref[...] = jnp.zeros_like(out_ref)
+    for s in range(got_ref.shape[0]):
+
+        @pl.when(valid_ref[s] > 0)
+        def _(s=s):
+            a = adapter_ref[s]
+            out_ref[a] = out_ref[a] + got_ref[s].astype(jnp.float32)
+
+
+def owner_sum(got, slot_adapter, slot_valid, adapters, tile):
+    slots, rank, width = got.shape
+    return pl.pallas_call(
+        owner_sum_kernel,
+        grid_spec=pltpu.PrefetchScalarGridSpec(
+            num_scalar_prefetch=2,
+            grid=(width // tile,),
+            in_specs=[pl.BlockSpec((slots, rank, tile), lambda i, a, v: (0, 0, i))],
+            out_specs=pl.BlockSpec((adapters, rank, tile), lambda i, a, v: (0, 0, i)),
+        ),
+        out_shape=jax.ShapeDtypeStruct((adapters, rank, width), jnp.float32),
+        compiler_params=pltpu.CompilerParams(vmem_limit_bytes=VMEM_LIMIT),
+        cost_estimate=pl.CostEstimate(
+            flops=slots * rank * width,
+            bytes_accessed=2 * slots * rank * width + 4 * adapters * rank * width,
+            transcendentals=0,
+        ),
+        name="owner_sum",
+    )(slot_adapter, slot_valid, got)
+
+
+def line_gather(own, me, n):
+    right = [(i, i + 1) for i in range(n - 1)]
+    from_left, from_right = [], []
+    a = b = own
+    for step in range(n - 1):
+        a = lax.ppermute(a, "tensor", [p for p in right if p[0] >= step])
+        b = lax.ppermute(b, "tensor", [(j, i) for i, j in right if j <= n - 1 - step])
+        from_left.append(a)
+        from_right.append(b)
+    parts = from_left[::-1] + [own] + from_right
+    rows = own.shape[0]
+    return lax.dynamic_slice_in_dim(jnp.concatenate(parts, axis=0), (n - 1 - me) * rows, n * rows, 0)
+
+
+def line_scatter(partial, me, n):
+    rows = partial.shape[0] // n
+
+    def piece(index):
+        return lax.dynamic_slice_in_dim(partial, jnp.clip(index, 0, n - 1) * rows, rows, 0)
+
+    mirrored = n - 1 - me
+    a = b = None
+    for step in range(n - 1):
+        send_a = piece(n - 1 - step + me)
+        send_b = piece(n - 1 - (n - 1 - step + mirrored))
+        if step > 0:
+            send_a = (send_a.astype(jnp.float32) + a.astype(jnp.float32)).astype(jnp.bfloat16)
+            send_b = (send_b.astype(jnp.float32) + b.astype(jnp.float32)).astype(jnp.bfloat16)
+        a = lax.ppermute(send_a, "tensor", [(i, i + 1) for i in range(n - 1) if i <= step])
+        b = lax.ppermute(
+            send_b, "tensor", [(n - 1 - i, n - 2 - i) for i in range(n - 1) if i <= step]
+        )
+    return piece(me).astype(jnp.float32) + a.astype(jnp.float32) + b.astype(jnp.float32)
+
+
+def local(
+    tokens,
+    frozen_key_weight,
+    adapter_down_maps,
+    adapter_up_maps,
+    cotangent,
+    block_owner_job,
+    block_local_adapter,
+    block_live_rows,
+):
+    own_rows = cotangent.shape[0]
+    if own_rows % BLOCK:
+        return general(
+            tokens,
+            frozen_key_weight,
+            adapter_down_maps,
+            adapter_up_maps,
+            cotangent,
+            block_owner_job,
+            block_local_adapter,
+            block_live_rows,
+        )
+    n = lax.axis_size("tensor")
+    me = lax.axis_index("tensor")
+    job_count = lax.axis_size("job")
+    own_job = lax.axis_index("job")
+    row_total = tokens.shape[0]
+    block_count = row_total // BLOCK
+    own_blocks = own_rows // BLOCK
+    adapters, width, rank = adapter_down_maps.shape
+    rank_portion, key_width = adapter_up_maps.shape[1:]
+    slots = job_count * SLOT_CAP
+
+    owners = block_owner_job[:, 0].reshape(job_count, block_count)
+    locals_all = block_local_adapter.reshape(job_count, block_count)
+    earlier = jnp.tril(jnp.ones((block_count, block_count), jnp.int32), -1)
+    place = jnp.sum((owners[:, :, None] == owners[:, None, :]) * earlier[None], axis=2)
+    slot_of = owners * SLOT_CAP + place
+    chosen = slot_of[:, None, :] == jnp.arange(slots, dtype=jnp.int32)[None, :, None]
+    slot_valid = jnp.sum(chosen, axis=2, dtype=jnp.int32)
+    slot_block = jnp.sum(chosen * jnp.arange(block_count, dtype=jnp.int32), axis=2)
+    slot_adapter = jnp.sum(chosen * locals_all[:, None, :], axis=2)
+
+    def of_job(table):
+        return lax.dynamic_index_in_dim(table, own_job, 0, keepdims=False)
+
+    def to_me(table):
+        split = table.reshape(job_count, job_count, SLOT_CAP)
+        return lax.dynamic_index_in_dim(split, own_job, 1, keepdims=False).reshape(slots)
+
+    my_slot, my_block, my_valid = of_job(slot_of), of_job(slot_block), of_job(slot_valid)
+    in_adapter, in_valid = to_me(slot_adapter), to_me(slot_valid)
+    my_fill = of_job(block_live_rows.reshape(job_count, block_count))
+    live = (jnp.arange(BLOCK, dtype=jnp.int32)[None, :] < my_fill[:, None]).astype(jnp.float32)
+    live_lanes = live.reshape(block_count, 1, BLOCK)
+    live_rows = live.reshape(row_total, 1)
+
+    def exchange(x):
+        shape = x.shape
+        return lax.all_to_all(
+            x.reshape((job_count, SLOT_CAP) + shape[1:]), "job", split_axis=0, concat_axis=0, tiled=True
+        ).reshape(shape)
+
+    def turn(x):
+        return lax.all_to_all(x, "tensor", split_axis=0, concat_axis=0, tiled=True)
+
+    down_t = jnp.transpose(adapter_down_maps, (0, 2, 1))
+    got_up = exchange(jnp.take(adapter_up_maps, in_adapter, axis=0))
+    got_down = exchange(jnp.take(down_t, in_adapter, axis=0))
+
+    cot_full = line_gather(cotangent, me, n)
+
+    up_blocks = jnp.take(got_up, my_slot, axis=0)
+    up_own = turn(up_blocks.reshape(n, own_blocks, rank_portion, key_width))
+    up_own = jnp.transpose(up_own, (1, 0, 2, 3)).reshape(own_blocks, rank, key_width)
+    cot_own = cotangent.reshape(own_blocks, BLOCK, key_width)
+    rank_grad_own = (
+        adapter_scale
+        * jnp.einsum("brd,bld->brl", up_own, cot_own, preferred_element_type=jnp.float32)
+    ).astype(jnp.bfloat16)
+    rank_grad = turn(jnp.broadcast_to(rank_grad_own[None], (n,) + rank_grad_own.shape))
+    rank_grad = rank_grad.reshape(block_count, rank, BLOCK)
+    rank_grad_live = rank_grad * live_lanes.astype(jnp.bfloat16)
+
+    got_terms = exchange(down_terms(tokens, rank_grad_live, my_block, my_valid))
+
+    partial = (
+        jnp.dot(tokens, frozen_key_weight, preferred_element_type=jnp.float32) * live_rows
+    ).astype(jnp.bfloat16)
+    base = line_scatter(partial, me, n)
+
+    rank_part = rank_partials(tokens, got_down, my_slot, live_lanes)
+    rank_sum = jnp.sum(
+        turn(rank_part.reshape(n, own_blocks, rank, BLOCK)).astype(jnp.float32), axis=0
+    ).astype(jnp.bfloat16)
+    adapter_rows = jnp.einsum("brl,brd->bld", rank_sum, up_own, preferred_element_type=jnp.float32)
+    projected = (base + adapter_scale * adapter_rows.reshape(own_rows, key_width)).astype(
+        jnp.bfloat16
+    )
+
+    rank_mine = turn(
+        jnp.transpose(rank_sum.reshape(own_blocks, n, rank_portion, BLOCK), (1, 0, 2, 3))
+    ).reshape(block_count, rank_portion, BLOCK)
+    up_terms = adapter_scale * jnp.einsum(
+        "bwl,blk->bwk",
+        rank_mine,
+        cot_full.reshape(block_count, BLOCK, key_width),
+        preferred_element_type=jnp.float32,
+    )
+    up_send = jnp.take(up_terms.astype(jnp.bfloat16), my_block, axis=0)
+    up_send = up_send * my_valid[:, None, None].astype(jnp.bfloat16)
+    got_up_terms = exchange(up_send)
+
+    grad_tokens = token_grads(
+        cot_full, frozen_key_weight, rank_grad, live_rows, got_down, my_slot, own_blocks
+    )
+    grad_down = owner_sum(got_terms, in_adapter, in_valid, adapters, min(width, 512))
+    grad_up = owner_sum(got_up_terms, in_adapter, in_valid, adapters, key_width)
+    return (projected, grad_tokens, jnp.transpose(grad_down, (0, 2, 1)), grad_up)
+
+
 def solution(mesh):
     placed = (
         P(("groups", "job"), "tensor"),

time: 310 us -> 235 us (0.76)
  the two profiles are of different devices: /device:TPU:0 before, /device:TPU:16 now
where the time goes in v1:
time: 235 us; the launch traced here: 233 us
  starting transfers between devices  72.5 us (31%)
  Pallas kernels  52.1 us (22%)
  waiting for transfers between devices  40.1 us (17%)
  local copies, waits for them, and re-layouts  32.7 us (14%)
  other arithmetic  21.1 us (9%)
  matrix products  13.4 us (6%)
    all_to_all x4, starting transfers between devices, turn(): return lax.all_to_all(x, 'tensor', split_axis=0, concat_axis=0, tiled=True)  24.1 us
    pallas_call x1, Pallas kernels, token_grads(): pl.pallas_call(functools.partial(grad_tokens_kernel, per_step), grid_spec...  22.8 us
    all_to_all x4, starting transfers between devices, exchange(): lax.all_to_all(x.reshape((job_count, SLOT_CAP) + shape[1:]), 'job', split...  17.3 us
    unnamed x29, local copies, waits for them, and re-layouts  15.8 us
    ppermute x3, waiting for transfers between devices, line_scatter(): lax.ppermute(send_b, 'tensor', [(n - 1 - i, n - 2 - i) for i in range(n -...  13.1 us
    ppermute x3, waiting for transfers between devices, line_gather(): lax.ppermute(b, 'tensor', [(j, i) for i, j in right if j <= n - 1 - step])  10.7 us
    pallas_call x1, Pallas kernels, rank_partials(): pl.pallas_call(rank_kernel, grid_spec=pltpu.PrefetchScalarGridSpec(num_sc...  10.6 us
    pallas_call x1, Pallas kernels, down_terms(): pl.pallas_call(down_terms_kernel, grid_spec=pltpu.PrefetchScalarGridSpec(...  10.5 us
  transfers between devices with their start and end apart: 20, of which 8 were waited for; matrix products, arithmetic and copies ran while one was open for 27% of the time, Pallas kernels for 20%

profile of v1, /device:TPU:16, one launch (start us, length us, event | category | flops | bytes accessed | tf_op | source)
XLA Modules:
  0.0 232.9 jit_solution(2315285778224968428)
XLA Ops:
  0.6 3.6 %collective-permute-start.6 = (bf16[384,1024]{1,0:T(8,128)(2,1)}, bf16[384,1024]{1,0:T(8,128)(2,1)}, u32[]{:S(2)}, u32[]{:S(2)}) collective-permute-start(bf16[384,1024]{1,0:T(8,128)(2,1)} %param.12), channel_id=1, source_target_pairs={{0,1},{1,2},{2,3},{4,5},{5,6},{6,7},{8,9},{9,10},{10,11},{12,13},{... | collective-permute-start | bytes 2359304 | tf_op jit(solution)/shard_map/ppermute | solution.py:284
  13.5 3.5 %all-to-all-start.2 = ((bf16[4,4,16,1024]{3,2,1,0:T(8,128)(2,1)}), bf16[4,4,16,1024]{3,2,1,0:T(8,128)(2,1)S(1)}, u32[]{:S(2)}, u32[]{:S(2)}) async-start(bf16[4,4,16,1024]{3,2,1,0:T(8,128)(2,1)} %broadcast_select_fusion.1), calls=%async_computation.2 | async-start | bytes 1048576 | tf_op jit(solution)/shard_map/all_to_all | solution.py:373
  17.3 2.8 %gather_fusion = bf16[16,64,2048]{2,1,0:T(8,128)(2,1)} fusion(bf16[8,64,2048]{2,1,0:T(8,128)(2,1)S(1)} %bitcast.63, s32[1024]{0:T(1024)S(1)} %pad_clamp_fusion.2), kind=kCustom, calls=%fused_computation | custom fusion | bytes 8388672 | tf_op jit(solution)/shard_map/jit(_take)/gather | solution.py:382
  20.3 5.5 %all-to-all-done.2 = bf16[4,4,16,1024]{3,2,1,0:T(8,128)(2,1)S(1)} async-done(((bf16[4,4,16,1024]{3,2,1,0:T(8,128)(2,1)}), bf16[4,4,16,1024]{3,2,1,0:T(8,128)(2,1)S(1)}, u32[]{:S(2)}, u32[]{:S(2)}) %all-to-all-start.2) | async-done | bytes 524320 | tf_op jit(solution)/shard_map/all_to_all | solution.py:373
  27.2 6.1 %all-to-all-start.3 = ((bf16[4,3,16,1024]{3,2,1,0:T(8,128)(2,1)}), bf16[4,3,16,1024]{3,2,1,0:T(8,128)(2,1)S(1)}, u32[]{:S(2)}, u32[]{:S(2)}) async-start(bf16[4,3,16,1024]{3,2,1,0:T(8,128)(2,1)} %broadcast_select_fusion.2), calls=%async_computation.3 | async-start | bytes 786432 | tf_op jit(solution)/shard_map/all_to_all | solution.py:378
  33.3 4.7 %broadcast_select_fusion = bf16[4,4,64,2048]{3,2,1,0:T(8,128)(2,1)} fusion(bf16[4,4,64,2048]{3,2,1,0:T(8,128)(2,1)} %bitcast.68, pred[4,4]{1,0:T(4,128)(4,1)S(1)} %get-tuple-element.19), kind=kLoop, calls=%fused_computation.5 | loop fusion | flops 2097152 | bytes 8388624 | tf_op jit(solution)/shard_map/jit(_take)/select_n | solution.py:382
  38.0 3.4 %collective-permute-start.7 = (bf16[384,1024]{1,0:T(8,128)(2,1)}, bf16[384,1024]{1,0:T(8,128)(2,1)}, u32[]{:S(2)}, u32[]{:S(2)}) collective-permute-start(bf16[384,1024]{1,0:T(8,128)(2,1)} %collective-permute-done.6), channel_id=1, source_target_pairs={{1,2},{2,3},{5,6},{6,7},{9,10},{10,11},{13,14},{14,15},{17,18},{18... | collective-permute-start | bytes 2359304 | tf_op jit(solution)/shard_map/ppermute | solution.py:284
  42.3 4.8 %all-to-all-start = ((bf16[4,4,64,2048]{3,2,1,0:T(8,128)(2,1)}), bf16[4,4,64,2048]{3,2,1,0:T(8,128)(2,1)}, u32[]{:S(2)}, u32[]{:S(2)}) async-start(bf16[4,4,64,2048]{3,2,1,0:T(8,128)(2,1)} %broadcast_select_fusion), calls=%async_computation | async-start | bytes 8388608 | tf_op jit(solution)/shard_map/all_to_all | solution.py:373
  47.1 10.0 %multiply_convert_fusion = bf16[1536,1024]{1,0:T(8,128)(2,1)S(1)} fusion(bf16[1536,2048]{1,0:T(8,128)(2,1)} %tokens_ref.3, bf16[2048,1024]{1,0:T(8,128)(2,1)} %weight_ref.1, f32[1536]{0:T(1024)S(1)} %get-tuple-element.17), kind=kOutput, calls=%fused_computation.4 | convolution fusion | flops 6445596672 | bytes 13637632 | tf_op jit(solution)/shard_map/dot_general | solution.py:401
  61.6 4.3 %collective-permute-start.10 = (bf16[384,1024]{1,0:T(8,128)(2,1)}, bf16[384,1024]{1,0:T(8,128)(2,1)}, u32[]{:S(2)}, u32[]{:S(2)}) collective-permute-start(bf16[384,1024]{1,0:T(8,128)(2,1)} %collective-permute-done.9), channel_id=1, source_target_pairs={{1,0},{2,1},{5,4},{6,5},{9,8},{10,9},{13,12},{14,13},{17,16},{18,1... | collective-permute-start | bytes 2359304 | tf_op jit(solution)/shard_map/ppermute | solution.py:285
  65.9 3.2 %collective-permute-start.8 = (bf16[384,1024]{1,0:T(8,128)(2,1)}, bf16[384,1024]{1,0:T(8,128)(2,1)S(1)}, u32[]{:S(2)}, u32[]{:S(2)}) collective-permute-start(bf16[384,1024]{1,0:T(8,128)(2,1)} %collective-permute-done.7), channel_id=1, source_target_pairs={{2,3},{6,7},{10,11},{14,15},{18,19},{22,23},{26,27},{30,31}} | collective-permute-start | bytes 2359304 | tf_op jit(solution)/shard_map/ppermute | solution.py:284
  72.0 10.7 %collective-permute-done.10 = bf16[384,1024]{1,0:T(8,128)(2,1)} collective-permute-done((bf16[384,1024]{1,0:T(8,128)(2,1)}, bf16[384,1024]{1,0:T(8,128)(2,1)}, u32[]{:S(2)}, u32[]{:S(2)}) %collective-permute-start.10) | collective-permute-done | bytes 786464 | tf_op jit(solution)/shard_map/ppermute | solution.py:285
  83.4 3.4 %collective-permute-done.8 = bf16[384,1024]{1,0:T(8,128)(2,1)S(1)} collective-permute-done((bf16[384,1024]{1,0:T(8,128)(2,1)}, bf16[384,1024]{1,0:T(8,128)(2,1)S(1)}, u32[]{:S(2)}, u32[]{:S(2)}) %collective-permute-start.8) | collective-permute-done | bytes 786464 | tf_op jit(solution)/shard_map/ppermute | solution.py:284
  92.7 2.6 %all-to-all-done = bf16[4,4,64,2048]{3,2,1,0:T(8,128)(2,1)} async-done(((bf16[4,4,64,2048]{3,2,1,0:T(8,128)(2,1)}), bf16[4,4,64,2048]{3,2,1,0:T(8,128)(2,1)}, u32[]{:S(2)}, u32[]{:S(2)}) %all-to-all-start) | async-done | bytes 4194336 | tf_op jit(solution)/shard_map/all_to_all | solution.py:373
  95.3 10.6 %rank_partials.1 = bf16[12,64,128]{2,1,0:T(8,128)(2,1)} custom-call(s32[12]{0:T(128)S(1)} %dynamic-slice_reduce_fusion.slot_ref, bf16[1536,2048]{1,0:T(8,128)(2,1)} %tokens_ref.3, bf16[16,64,2048]{2,1,0:T(8,128)(2,1)} %bitcast.6.down_ref.rest_0_.rest_1_.rest_2_, f32[12,1,128]{2,1,0:T(1,128)S(1)} %compare_convert_fusion.live_ref), custom_call_target="tpu_custom_call" | custom-call | flops 402653184 | bytes 9437184 | tf_op jit(solution)/shard_map/rank_partials/pallas_call | solution.py:140
  105.9 6.6 %all-to-all-start.1 = ((bf16[4,3,64,128]{3,2,1,0:T(8,128)(2,1)}), bf16[4,3,64,128]{3,2,1,0:T(8,128)(2,1)S(1)}, u32[]{:S(2)}, u32[]{:S(2)}) async-start(bf16[4,3,64,128]{3,2,1,0:T(8,128)(2,1)} %bitcast.7), calls=%async_computation.1 | async-start | bytes 393216 | tf_op jit(solution)/shard_map/all_to_all | solution.py:378
  118.3 5.8 %all-to-all-start.6 = ((bf16[4,3,16,128]{3,2,1,0:T(8,128)(2,1)}), bf16[4,3,16,128]{3,2,1,0:T(8,128)(2,1)S(1)}, u32[]{:S(2)}, u32[]{:S(2)}) async-start(bf16[4,3,16,128]{3,2,1,0:T(8,128)(2,1)} %bitcast.61), calls=%async_computation.6 | async-start | bytes 98304 | tf_op jit(solution)/shard_map/all_to_all | solution.py:378
  128.2 5.6 %all-to-all-start.4 = ((bf16[4,3,64,128]{3,2,1,0:T(8,128)(2,1)}), bf16[4,3,64,128]{3,2,1,0:T(8,128)(2,1)S(1)}, u32[]{:S(2)}, u32[]{:S(2)}) async-start(bf16[4,3,64,128]{3,2,1,0:T(8,128)(2,1)} %broadcast_in_dim.66), calls=%async_computation.4 | async-start | bytes 393216 | tf_op jit(solution)/shard_map/all_to_all | solution.py:378
  139.4 4.1 %all-to-all-start.7 = ((bf16[4,4,16,1024]{3,2,1,0:T(8,128)(2,1)}), bf16[4,4,16,1024]{3,2,1,0:T(8,128)(2,1)}, u32[]{:S(2)}, u32[]{:S(2)}) async-start(bf16[4,4,16,1024]{3,2,1,0:T(8,128)(2,1)} %select_multiply_fusion), calls=%async_computation.7 | async-start | bytes 1048576 | tf_op jit(solution)/shard_map/all_to_all | solution.py:373
  143.6 2.6 %add_convert_fusion.3 = bf16[384,1024]{1,0:T(8,128)(2,1)} fusion(bf16[384,1024]{1,0:T(8,128)(2,1)} %collective-permute-done, bf16[1536,1024]{1,0:T(8,128)(2,1)} %copy-done.4, s32[]{:T(128)S(6)} %select_n.118), kind=kLoop, calls=%fused_computation.11 | loop fusion | flops 1572864 | bytes 2359300 | tf_op jit(solution)/shard_map/convert_element_type | solution.py:305
  147.5 10.5 %down_terms.1 = bf16[16,64,2048]{2,1,0:T(8,128)(2,1)S(1)} custom-call(s32[16]{0:T(128)S(1)} %get-tuple-element.14.block_ref, s32[16]{0:T(128)S(1)} %fusion.9.valid_ref, bf16[1536,2048]{1,0:T(8,128)(2,1)} %tokens_ref.3, bf16[12,64,128]{2,1,0:T(8,128)(2,1)S(1)} %broadcast_multiply_fusion.rank_grad_ref), custom_call_target="tpu_custom_call" | custom-call | flops 536870912 | bytes 12582912 | tf_op jit(solution)/shard_map/down_terms/pallas_call | solution.py:226
  160.0 4.8 %all-to-all-start.5 = ((bf16[4,4,64,2048]{3,2,1,0:T(8,128)(2,1)}), bf16[4,4,64,2048]{3,2,1,0:T(8,128)(2,1)}, u32[]{:S(2)}, u32[]{:S(2)}) async-start(bf16[4,4,64,2048]{3,2,1,0:T(8,128)(2,1)} %bitcast.65), calls=%async_computation.5 | async-start | bytes 8388608 | tf_op jit(solution)/shard_map/all_to_all | solution.py:373
  164.8 3.4 %collective-permute-done.1 = bf16[384,1024]{1,0:T(8,128)(2,1)} collective-permute-done((bf16[384,1024]{1,0:T(8,128)(2,1)}, bf16[384,1024]{1,0:T(8,128)(2,1)}, u32[]{:S(2)}, u32[]{:S(2)}) %collective-permute-start.1) | collective-permute-done | bytes 786464 | tf_op jit(solution)/shard_map/ppermute | solution.py:307
  168.2 3.7 %add_convert_fusion.2 = (bf16[384,1024]{1,0:T(8,128)(2,1)}, bf16[384,1024]{1,0:T(8,128)(2,1)}) fusion(bf16[384,1024]{1,0:T(8,128)(2,1)} %collective-permute-done.1, bf16[1536,1024]{1,0:T(8,128)(2,1)} %copy-done.4, s32[]{:T(128)S(6)} %select_n.117, bf16[384,1024]{1,0:T(8,128)(2,1)} %collective-permute-done.3, s32[]{:T(128)S(6)} %select_n.121), kind=kLoop, calls=%fused_computation.10 | loop fusion | flops 3145728 | bytes 4718600 | tf_op jit(solution)/shard_map/convert_element_type | solution.py:305
  171.9 2.5 %collective-permute-start.4 = (bf16[384,1024]{1,0:T(8,128)(2,1)}, bf16[384,1024]{1,0:T(8,128)(2,1)}, u32[]{:S(2)}, u32[]{:S(2)}) collective-permute-start(bf16[384,1024]{1,0:T(8,128)(2,1)} %get-tuple-element.10), channel_id=1, source_target_pairs={{3,2},{2,1},{7,6},{6,5},{11,10},{10,9},{15,14},{14,13},{19,18},{18... | collective-permute-start | bytes 2359304 | tf_op jit(solution)/shard_map/ppermute | solution.py:308
  175.9 4.2 %collective-permute-start.2 = (bf16[384,1024]{1,0:T(8,128)(2,1)}, bf16[384,1024]{1,0:T(8,128)(2,1)S(1)}, u32[]{:S(2)}, u32[]{:S(2)}) collective-permute-start(bf16[384,1024]{1,0:T(8,128)(2,1)} %get-tuple-element.9), channel_id=1, source_target_pairs={{0,1},{1,2},{2,3},{4,5},{5,6},{6,7},{8,9},{9,10},{10,11},{12,13},{... | collective-permute-start | bytes 2359304 | tf_op jit(solution)/shard_map/ppermute | solution.py:307
  180.1 13.1 %collective-permute-done.4 = bf16[384,1024]{1,0:T(8,128)(2,1)} collective-permute-done((bf16[384,1024]{1,0:T(8,128)(2,1)}, bf16[384,1024]{1,0:T(8,128)(2,1)}, u32[]{:S(2)}, u32[]{:S(2)}) %collective-permute-start.4) | collective-permute-done | bytes 786464 | tf_op jit(solution)/shard_map/ppermute | solution.py:308
  194.9 2.7 %collective-permute-start.5 = (bf16[384,1024]{1,0:T(8,128)(2,1)S(1)}, bf16[384,1024]{1,0:T(8,128)(2,1)S(1)}, u32[]{:S(2)}, u32[]{:S(2)}) collective-permute-start(bf16[384,1024]{1,0:T(8,128)(2,1)S(1)} %add_convert_fusion), channel_id=1, source_target_pairs={{3,2},{2,1},{1,0},{7,6},{6,5},{5,4},{11,10},{10,9},{9,8},{15,14},{... | collective-permute-start | bytes 2359304 | tf_op jit(solution)/shard_map/ppermute | solution.py:308
  198.7 22.8 %token_grads.1 = bf16[1536,2048]{1,0:T(8,128)(2,1)} custom-call(s32[12]{0:T(128)S(1)} %dynamic-slice_reduce_fusion.slot_ref, bf16[1536,1024]{1,0:T(8,128)(2,1)S(1)} %constant_dynamic-slice_fusion.2.cot_ref, bf16[2048,1024]{1,0:T(8,128)(2,1)} %weight_ref.1, bf16[12,64,128]{2,1,0:T(8,128)(2,1)S(1)} %bitcast.67, f32[1536,1]{1,0:T(8,128)S(1)} %bitcast.66, ...), custom_call_target="tpu_custom_call" | custom-call | flops 6845104128 | bytes 13631488 | tf_op jit(solution)/shard_map/token_grads/pallas_call | solution.py:177
  221.9 2.6 %fusion = bf16[384,1024]{1,0:T(8,128)(2,1)} fusion(f32[3,128,1024]{2,1,0:T(8,128)S(1)} %convolution_multiply_fusion, bf16[384,1024]{1,0:T(8,128)(2,1)S(1)} %collective-permute-done.5, bf16[384,1024]{1,0:T(8,128)(2,1)S(1)} %collective-permute-done.2, bf16[1536,1024]{1,0:T(8,128)(2,1)} %copy-done.4, s32[]{:T(128)S(6)} %select_n.116), kind=kLoop, calls=%fused_computation.7 | loop fusion | flops 2752512 | bytes 4718596 | tf_op jit(solution)/shard_map/convert_element_type | solution.py:410
  224.6 2.6 %owner_sum.3 = f32[8,16,1024]{2,1,0:T(8,128)} custom-call(s32[16]{0:T(128)S(1)} %reshape.327.adapter_ref, s32[16]{0:T(128)S(1)} %reshape.329.valid_ref, bf16[16,16,1024]{2,1,0:T(8,128)(2,1)} %bitcast.29.got_ref), custom_call_target="tpu_custom_call" | custom-call | flops 262144 | bytes 1048576 | tf_op jit(solution)/shard_map/owner_sum/pallas_call | solution.py:260
  227.1 5.7 %owner_sum.2 = f32[8,64,2048]{2,1,0:T(8,128)} custom-call(s32[16]{0:T(128)S(1)} %reshape.327.adapter_ref, s32[16]{0:T(128)S(1)} %reshape.329.valid_ref, bf16[16,64,2048]{2,1,0:T(8,128)(2,1)} %bitcast.20.got_ref), custom_call_target="tpu_custom_call" | custom-call | flops 2097152 | bytes 8388608 | tf_op jit(solution)/shard_map/owner_sum/pallas_call | solution.py:260
  (102 shorter events, 49.4 us)
Async XLA Ops:
  0.6 16.6 %copy-start = (bf16[8,2048,64]{1,2,0:T(8,128)(2,1)S(1)}, bf16[8,2048,64]{1,2,0:T(8,128)(2,1)}, u32[]{:S(2)}) copy-start(bf16[8,2048,64]{1,2,0:T(8,128)(2,1)} %param.10) | copy-start | bytes 6291460
  0.6 37.3 %collective-permute-start.6 = (bf16[384,1024]{1,0:T(8,128)(2,1)}, bf16[384,1024]{1,0:T(8,128)(2,1)}, u32[]{:S(2)}, u32[]{:S(2)}) collective-permute-start(bf16[384,1024]{1,0:T(8,128)(2,1)} %param.12), channel_id=1, source_target_pairs={{0,1},{1,2},{2,3},{4,5},{5,6},{6,7},{8,9},{9,10},{10,11},{12,13},{... | collective-permute-start | bytes 2359304 | tf_op jit(solution)/shard_map/ppermute | solution.py:284
  4.3 57.3 %collective-permute-start.9 = (bf16[384,1024]{1,0:T(8,128)(2,1)}, bf16[384,1024]{1,0:T(8,128)(2,1)}, u32[]{:S(2)}, u32[]{:S(2)}) collective-permute-start(bf16[384,1024]{1,0:T(8,128)(2,1)} %param.12), channel_id=1, source_target_pairs={{1,0},{2,1},{3,2},{5,4},{6,5},{7,6},{9,8},{10,9},{11,10},{13,12},{... | collective-permute-start | bytes 2359304 | tf_op jit(solution)/shard_map/ppermute | solution.py:285
  13.5 12.3 %all-to-all-start.2 = ((bf16[4,4,16,1024]{3,2,1,0:T(8,128)(2,1)}), bf16[4,4,16,1024]{3,2,1,0:T(8,128)(2,1)S(1)}, u32[]{:S(2)}, u32[]{:S(2)}) async-start(bf16[4,4,16,1024]{3,2,1,0:T(8,128)(2,1)} %broadcast_select_fusion.1), calls=%async_computation.2 | async-start | bytes 1048576 | tf_op jit(solution)/shard_map/all_to_all | solution.py:373
  17.2 2.8 %copy-start.9 = (s32[48]{0:T(128)S(1)}, s32[48]{0:T(128)}, u32[]{:S(2)}) copy-start(s32[48]{0:T(128)} %param.15) | copy-start | bytes 580
  27.2 14.3 %all-to-all-start.3 = ((bf16[4,3,16,1024]{3,2,1,0:T(8,128)(2,1)}), bf16[4,3,16,1024]{3,2,1,0:T(8,128)(2,1)S(1)}, u32[]{:S(2)}, u32[]{:S(2)}) async-start(bf16[4,3,16,1024]{3,2,1,0:T(8,128)(2,1)} %broadcast_select_fusion.2), calls=%async_computation.3 | async-start | bytes 786432 | tf_op jit(solution)/shard_map/all_to_all | solution.py:378
  38.0 27.9 %collective-permute-start.7 = (bf16[384,1024]{1,0:T(8,128)(2,1)}, bf16[384,1024]{1,0:T(8,128)(2,1)}, u32[]{:S(2)}, u32[]{:S(2)}) collective-permute-start(bf16[384,1024]{1,0:T(8,128)(2,1)} %collective-permute-done.6), channel_id=1, source_target_pairs={{1,2},{2,3},{5,6},{6,7},{9,10},{10,11},{13,14},{14,15},{17,18},{18... | collective-permute-start | bytes 2359304 | tf_op jit(solution)/shard_map/ppermute | solution.py:284
  41.5 0.7 copy-start.8
  42.3 53.1 %all-to-all-start = ((bf16[4,4,64,2048]{3,2,1,0:T(8,128)(2,1)}), bf16[4,4,64,2048]{3,2,1,0:T(8,128)(2,1)}, u32[]{:S(2)}, u32[]{:S(2)}) async-start(bf16[4,4,64,2048]{3,2,1,0:T(8,128)(2,1)} %broadcast_select_fusion), calls=%async_computation | async-start | bytes 8388608 | tf_op jit(solution)/shard_map/all_to_all | solution.py:373
  57.1 12.0 %copy-start.4 = (bf16[1536,1024]{1,0:T(8,128)(2,1)}, bf16[1536,1024]{1,0:T(8,128)(2,1)S(1)}, u32[]{:S(2)}) copy-start(bf16[1536,1024]{1,0:T(8,128)(2,1)S(1)} %multiply_convert_fusion) | copy-start | bytes 9437188
  58.6 85.0 %collective-permute-start = (bf16[384,1024]{1,0:T(8,128)(2,1)}, bf16[384,1024]{1,0:T(8,128)(2,1)}, u32[]{:S(2)}, u32[]{:S(2)}) collective-permute-start(bf16[384,1024]{1,0:T(8,128)(2,1)} %get-tuple-element.11), channel_id=1, source_target_pairs={{0,1},{4,5},{8,9},{12,13},{16,17},{20,21},{24,25},{28,29}} | collective-permute-start | bytes 2359304 | tf_op jit(solution)/shard_map/ppermute | solution.py:307
  60.1 104.7 %collective-permute-start.3 = (bf16[384,1024]{1,0:T(8,128)(2,1)}, bf16[384,1024]{1,0:T(8,128)(2,1)}, u32[]{:S(2)}, u32[]{:S(2)}) collective-permute-start(bf16[384,1024]{1,0:T(8,128)(2,1)} %get-tuple-element.12), channel_id=1, source_target_pairs={{3,2},{7,6},{11,10},{15,14},{19,18},{23,22},{27,26},{31,30}} | collective-permute-start | bytes 2359304 | tf_op jit(solution)/shard_map/ppermute | solution.py:308
  61.5 30.3 %copy-start.7 = (bf16[384,1024]{1,0:T(8,128)(2,1)S(1)}, bf16[384,1024]{1,0:T(8,128)(2,1)}, u32[]{:S(2)}) copy-start(bf16[384,1024]{1,0:T(8,128)(2,1)} %param.12) | copy-start | bytes 2359300
  61.6 21.1 %collective-permute-start.10 = (bf16[384,1024]{1,0:T(8,128)(2,1)}, bf16[384,1024]{1,0:T(8,128)(2,1)}, u32[]{:S(2)}, u32[]{:S(2)}) collective-permute-start(bf16[384,1024]{1,0:T(8,128)(2,1)} %collective-permute-done.9), channel_id=1, source_target_pairs={{1,0},{2,1},{5,4},{6,5},{9,8},{10,9},{13,12},{14,13},{17,16},{18,1... | collective-permute-start | bytes 2359304 | tf_op jit(solution)/shard_map/ppermute | solution.py:285
  65.9 20.9 %collective-permute-start.8 = (bf16[384,1024]{1,0:T(8,128)(2,1)}, bf16[384,1024]{1,0:T(8,128)(2,1)S(1)}, u32[]{:S(2)}, u32[]{:S(2)}) collective-permute-start(bf16[384,1024]{1,0:T(8,128)(2,1)} %collective-permute-done.7), channel_id=1, source_target_pairs={{2,3},{6,7},{10,11},{14,15},{18,19},{22,23},{26,27},{30,31}} | collective-permute-start | bytes 2359304 | tf_op jit(solution)/shard_map/ppermute | solution.py:284
  70.3 35.6 %copy-start.5 = (bf16[3,4,16,1024]{3,2,1,0:T(8,128)(2,1)}, bf16[3,4,16,1024]{3,2,1,0:T(8,128)(2,1)S(1)}, u32[]{:S(2)}) copy-start(bf16[3,4,16,1024]{3,2,1,0:T(8,128)(2,1)S(1)} %copy.26) | copy-start | bytes 1179652
  82.7 34.0 %collective-permute-start.11 = (bf16[384,1024]{1,0:T(8,128)(2,1)}, bf16[384,1024]{1,0:T(8,128)(2,1)S(1)}, u32[]{:S(2)}, u32[]{:S(2)}) collective-permute-start(bf16[384,1024]{1,0:T(8,128)(2,1)} %collective-permute-done.10), channel_id=1, source_target_pairs={{1,0},{5,4},{9,8},{13,12},{17,16},{21,20},{25,24},{29,28}} | collective-permute-start | bytes 2359304 | tf_op jit(solution)/shard_map/ppermute | solution.py:285
  105.9 11.7 %all-to-all-start.1 = ((bf16[4,3,64,128]{3,2,1,0:T(8,128)(2,1)}), bf16[4,3,64,128]{3,2,1,0:T(8,128)(2,1)S(1)}, u32[]{:S(2)}, u32[]{:S(2)}) async-start(bf16[4,3,64,128]{3,2,1,0:T(8,128)(2,1)} %bitcast.7), calls=%async_computation.1 | async-start | bytes 393216 | tf_op jit(solution)/shard_map/all_to_all | solution.py:378
  118.3 9.2 %all-to-all-start.6 = ((bf16[4,3,16,128]{3,2,1,0:T(8,128)(2,1)}), bf16[4,3,16,128]{3,2,1,0:T(8,128)(2,1)S(1)}, u32[]{:S(2)}, u32[]{:S(2)}) async-start(bf16[4,3,16,128]{3,2,1,0:T(8,128)(2,1)} %bitcast.61), calls=%async_computation.6 | async-start | bytes 98304 | tf_op jit(solution)/shard_map/all_to_all | solution.py:378
  128.2 11.2 %all-to-all-start.4 = ((bf16[4,3,64,128]{3,2,1,0:T(8,128)(2,1)}), bf16[4,3,64,128]{3,2,1,0:T(8,128)(2,1)S(1)}, u32[]{:S(2)}, u32[]{:S(2)}) async-start(bf16[4,3,64,128]{3,2,1,0:T(8,128)(2,1)} %broadcast_in_dim.66), calls=%async_computation.4 | async-start | bytes 393216 | tf_op jit(solution)/shard_map/all_to_all | solution.py:378
  139.4 20.6 %all-to-all-start.7 = ((bf16[4,4,16,1024]{3,2,1,0:T(8,128)(2,1)}), bf16[4,4,16,1024]{3,2,1,0:T(8,128)(2,1)}, u32[]{:S(2)}, u32[]{:S(2)}) async-start(bf16[4,4,16,1024]{3,2,1,0:T(8,128)(2,1)} %select_multiply_fusion), calls=%async_computation.7 | async-start | bytes 1048576 | tf_op jit(solution)/shard_map/all_to_all | solution.py:373
  146.1 22.1 %collective-permute-start.1 = (bf16[384,1024]{1,0:T(8,128)(2,1)}, bf16[384,1024]{1,0:T(8,128)(2,1)}, u32[]{:S(2)}, u32[]{:S(2)}) collective-permute-start(bf16[384,1024]{1,0:T(8,128)(2,1)} %add_convert_fusion.3), channel_id=1, source_target_pairs={{0,1},{1,2},{4,5},{5,6},{8,9},{9,10},{12,13},{13,14},{16,17},{17,1... | collective-permute-start | bytes 2359304 | tf_op jit(solution)/shard_map/ppermute | solution.py:307
  157.9 2.0 copy-start.2
  160.0 67.2 %all-to-all-start.5 = ((bf16[4,4,64,2048]{3,2,1,0:T(8,128)(2,1)}), bf16[4,4,64,2048]{3,2,1,0:T(8,128)(2,1)}, u32[]{:S(2)}, u32[]{:S(2)}) async-start(bf16[4,4,64,2048]{3,2,1,0:T(8,128)(2,1)} %bitcast.65), calls=%async_computation.5 | async-start | bytes 8388608 | tf_op jit(solution)/shard_map/all_to_all | solution.py:373
  171.9 21.3 %collective-permute-start.4 = (bf16[384,1024]{1,0:T(8,128)(2,1)}, bf16[384,1024]{1,0:T(8,128)(2,1)}, u32[]{:S(2)}, u32[]{:S(2)}) collective-permute-start(bf16[384,1024]{1,0:T(8,128)(2,1)} %get-tuple-element.10), channel_id=1, source_target_pairs={{3,2},{2,1},{7,6},{6,5},{11,10},{10,9},{15,14},{14,13},{19,18},{18... | collective-permute-start | bytes 2359304 | tf_op jit(solution)/shard_map/ppermute | solution.py:308
  175.9 46.0 %collective-permute-start.2 = (bf16[384,1024]{1,0:T(8,128)(2,1)}, bf16[384,1024]{1,0:T(8,128)(2,1)S(1)}, u32[]{:S(2)}, u32[]{:S(2)}) collective-permute-start(bf16[384,1024]{1,0:T(8,128)(2,1)} %get-tuple-element.9), channel_id=1, source_target_pairs={{0,1},{1,2},{2,3},{4,5},{5,6},{6,7},{8,9},{9,10},{10,11},{12,13},{... | collective-permute-start | bytes 2359304 | tf_op jit(solution)/shard_map/ppermute | solution.py:307
  194.9 27.1 %collective-permute-start.5 = (bf16[384,1024]{1,0:T(8,128)(2,1)S(1)}, bf16[384,1024]{1,0:T(8,128)(2,1)S(1)}, u32[]{:S(2)}, u32[]{:S(2)}) collective-permute-start(bf16[384,1024]{1,0:T(8,128)(2,1)S(1)} %add_convert_fusion), channel_id=1, source_target_pairs={{3,2},{2,1},{1,0},{7,6},{6,5},{5,4},{11,10},{10,9},{9,8},{15,14},{... | collective-permute-start | bytes 2359304 | tf_op jit(solution)/shard_map/ppermute | solution.py:308
  197.6 1.1 copy-start.3
  198.7 22.8 %copy-start.6 = (bf16[3,4,16,1024]{3,2,1,0:T(8,128)(2,1)S(1)}, bf16[3,4,16,1024]{3,2,1,0:T(8,128)(2,1)}, u32[]{:S(2)}) copy-start(bf16[3,4,16,1024]{3,2,1,0:T(8,128)(2,1)} %copy-done.5) | copy-start | bytes 1179652
  227.1 5.7 %copy-start.1 = (bf16[8,2048,64]{1,2,0:T(8,128)(2,1)S(1)}, bf16[8,2048,64]{1,2,0:T(8,128)(2,1)}, u32[]{:S(2)}) copy-start(bf16[8,2048,64]{1,2,0:T(8,128)(2,1)} %param.10) | copy-start | bytes 6291460

commit v2 on v0

--- a/solution.py
+++ b/solution.py
@@ -1,15 +1,28 @@
+import functools
+
 import jax
 import jax.numpy as jnp
 from jax import lax
+from jax.experimental import pallas as pl
+from jax.experimental.pallas import tpu as pltpu
 from jax.sharding import PartitionSpec as P
 
 BLOCK = 128
+SLOT_CAP = 4
+VMEM_LIMIT = 48 * 1024 * 1024
 
 
 adapter_scale = 2.0
 
-
-def local(
+NT = (((1,), (1,)), ((), ()))
+TN = (((0,), (0,)), ((), ()))
+
+
+def dot(a, b, dims):
+    return lax.dot_general(a, b, dims, preferred_element_type=jnp.float32)
+
+
+def general(
     tokens,
     frozen_key_weight,
     adapter_down_maps,
@@ -115,6 +128,601 @@
     return (projected, grad_tokens, grad_down, grad_up)
 
 
+def peers_of(own, groups):
+    x, core = own // 2, own % 2
+    return (2 * (1 - x) + core, 2 * (1 - x) + 1 - core, 2 * x + 1 - core)
+
+
+def main_kernel(
+    n,
+    owner_ref,
+    local_ref,
+    fill_ref,
+    tokens_in,
+    weight_in,
+    down_in,
+    up_in,
+    cot_in,
+    projected_ref,
+    grad_tokens_out,
+    got_terms,
+    got_up_terms,
+    tokens,
+    weight,
+    down_all,
+    up_all,
+    cot,
+    part,
+    from_left,
+    from_right,
+    up_turn,
+    up_own,
+    rank_grad,
+    rank_part,
+    rank_in,
+    rank_split,
+    rank_mine,
+    term_send,
+    up_term_send,
+    staged,
+    load_sem,
+    send_sem,
+    recv_sem,
+):
+    group = lax.axis_index("groups")
+    job = lax.axis_index("job")
+    me = lax.axis_index("tensor")
+    blocks = tokens.shape[0]
+    own_blocks = blocks // n
+    width = tokens.shape[2]
+    key_width = weight.shape[1]
+    adapters = down_in.shape[0]
+    rank = down_in.shape[1]
+    portion = rank // n
+    jobs = 4
+    half = adapters // 2
+    jx, jd, js = peers_of(job, None)
+    counter = [0]
+    loads = [0]
+
+    def remote(src, dst, where):
+        k = counter[0]
+        counter[0] += 1
+        return pltpu.make_async_remote_copy(
+            src_ref=src,
+            dst_ref=dst,
+            send_sem=send_sem.at[k],
+            recv_sem=recv_sem.at[k],
+            device_id=where,
+            device_id_type=pl.DeviceIdType.MESH,
+        )
+
+    def load(src, dst):
+        k = loads[0]
+        loads[0] += 1
+        copy = pltpu.make_async_copy(src, dst, load_sem.at[k])
+        copy.start()
+        return copy
+
+    others = [lax.rem(me + r, n) for r in range(1, n)]
+
+    own_slice = pl.ds(me * own_blocks, own_blocks)
+    cot_load = load(cot_in, cot.at[own_slice])
+    weight_load = load(weight_in, weight)
+    tokens_load = load(tokens_in, tokens)
+    up_load = load(up_in, up_all.at[pl.ds(job * adapters, adapters)])
+    down_load = load(down_in, down_all.at[pl.ds(job * adapters, adapters)])
+
+    barrier = pltpu.get_barrier_semaphore()
+    for p in (jx, jd, js):
+        pl.semaphore_signal(
+            barrier, inc=1, device_id={"job": p}, device_id_type=pl.DeviceIdType.MESH
+        )
+    for p in others:
+        pl.semaphore_signal(
+            barrier, inc=1, device_id={"tensor": p}, device_id_type=pl.DeviceIdType.MESH
+        )
+    pl.semaphore_signal(
+        barrier, inc=1, device_id={"groups": 1 - group}, device_id_type=pl.DeviceIdType.MESH
+    )
+    pl.semaphore_wait(barrier, 3 + len(others) + 1)
+
+    up_copies = [
+        remote(up_in, up_all.at[pl.ds(job * adapters, adapters)], {"job": p}) for p in (jx, jd, js)
+    ]
+    for c in up_copies:
+        c.start()
+
+    def chunk(index):
+        return pl.ds(index * own_blocks, own_blocks)
+
+    right_gather, left_gather = [], []
+    for s in range(n - 1):
+        rs, ls = jnp.clip(me - s, 0, n - 1), jnp.clip(me + s, 0, n - 1)
+        right_gather.append(
+            remote(
+                cot_in if s == 0 else cot.at[chunk(rs)],
+                cot.at[chunk(rs)],
+                {"tensor": jnp.minimum(me + 1, n - 1)},
+            )
+        )
+        left_gather.append(
+            remote(
+                cot_in if s == 0 else cot.at[chunk(ls)],
+                cot.at[chunk(ls)],
+                {"tensor": jnp.maximum(me - 1, 0)},
+            )
+        )
+
+    def gather_send(s):
+        @pl.when((me >= s) & (me <= n - 2))
+        def _():
+            right_gather[s].start()
+
+        @pl.when((me <= n - 1 - s) & (me >= 1))
+        def _():
+            left_gather[s].start()
+
+    def gather_recv(s):
+        @pl.when(me - 1 >= s)
+        def _():
+            right_gather[s].wait_recv()
+
+        @pl.when(me + 1 <= n - 1 - s)
+        def _():
+            left_gather[s].wait_recv()
+
+    gather_send(0)
+
+    def region(owner, h):
+        return down_all.at[pl.ds(owner * adapters + h * half, half)]
+
+    copy_a = remote(down_in.at[pl.ds(group * half, half)], region(job, group), {"job": jx})
+    copy_b = remote(down_in, down_all.at[pl.ds(job * adapters, adapters)], {"job": js})
+    copy_c = remote(region(jx, group), region(jx, group), {"groups": 1 - group})
+    copy_d = remote(region(jx, group), region(jx, group), {"job": js})
+    copy_e = remote(region(jx, 1 - group), region(jx, 1 - group), {"job": js})
+    copy_a.start()
+    copy_b.start()
+
+    base = job * blocks
+    owner = [owner_ref[base + b] for b in range(blocks)]
+    adapter = [owner[b] * adapters + local_ref[base + b] for b in range(blocks)]
+    fill = [fill_ref[base + b] for b in range(blocks)]
+    place = []
+    for b in range(blocks):
+        total = jnp.int32(0)
+        for e in range(b):
+            total = total + jnp.where(owner[e] == owner[b], 1, 0)
+        place.append(total)
+
+    def slot(o, s):
+        index, valid = jnp.int32(0), jnp.int32(0)
+        for b in range(blocks):
+            hit = jnp.where((owner[b] == o) & (place[b] == s), 1, 0)
+            index, valid = index + b * hit, valid + hit
+        return index, valid
+
+    def live_column(b):
+        return lax.broadcasted_iota(jnp.int32, (BLOCK, 1), 0) < fill[b]
+
+    def live_row(b):
+        return lax.broadcasted_iota(jnp.int32, (1, BLOCK), 1) < fill[b]
+
+    weight_load.wait()
+    tokens_load.wait()
+    tile = 256
+    per = blocks // 2
+    for h in range(2):
+        masks = [live_column(h * per + k) for k in range(per)]
+
+        @pl.loop(0, key_width // tile)
+        def _(t, h=h, masks=masks):
+            columns = pl.ds(pl.multiple_of(t * tile, tile), tile)
+            rows = tokens[pl.ds(h * per, per)].reshape(per * BLOCK, width)
+            acc = jnp.dot(rows, weight[:, columns], preferred_element_type=jnp.float32)
+            for k in range(per):
+                part[h * per + k, :, columns] = jnp.where(
+                    masks[k], acc[k * BLOCK : (k + 1) * BLOCK], 0.0
+                ).astype(part.dtype)
+
+    up_load.wait()
+    for c in up_copies:
+        c.wait_recv()
+    turn_copies = [
+        remote(up_turn.at[p], up_own.at[me], {"tensor": p}) for p in others
+    ]
+    for b in range(blocks):
+        up_turn[b // own_blocks, b % own_blocks] = up_all[adapter[b]]
+    for c in turn_copies:
+        c.start()
+    up_own[me] = up_turn[me]
+
+    cot_load.wait()
+    gather_recv(0)
+    gather_send(1)
+
+    right_sum, left_sum = [], []
+    for s in range(n - 1):
+        rd = jnp.clip(n - 1 - s + me, 0, n - 1)
+        ld = jnp.clip(s - (n - 1 - me), 0, n - 1)
+        right_sum.append(
+            (
+                rd,
+                remote(
+                    part.at[chunk(rd)], from_left.at[s], {"tensor": jnp.minimum(me + 1, n - 1)}
+                ),
+            )
+        )
+        left_sum.append(
+            (
+                ld,
+                remote(part.at[chunk(ld)], from_right.at[s], {"tensor": jnp.maximum(me - 1, 0)}),
+            )
+        )
+
+    def add_into(index, got):
+        for k in range(own_blocks):
+            b = index * own_blocks + k
+            part[b] = (part[b].astype(jnp.float32) + got[k].astype(jnp.float32)).astype(part.dtype)
+
+    def sum_send(s):
+        mirrored = n - 1 - me
+
+        @pl.when((me <= s) & (me <= n - 2))
+        def _():
+            index, copy = right_sum[s]
+            if s > 0:
+
+                @pl.when(me >= 1)
+                def _():
+                    right_sum[s - 1][1].wait_recv()
+                    add_into(index, from_left.at[s - 1])
+
+            copy.start()
+
+        @pl.when((mirrored <= s) & (mirrored <= n - 2))
+        def _():
+            index, copy = left_sum[s]
+            if s > 0:
+
+                @pl.when(mirrored >= 1)
+                def _():
+                    left_sum[s - 1][1].wait_recv()
+                    add_into(index, from_right.at[s - 1])
+
+            copy.start()
+
+    sum_send(0)
+
+    for c in turn_copies:
+        c.wait_recv()
+    up_full = [up_own[:, k].reshape(rank, key_width) for k in range(own_blocks)]
+    for k in range(own_blocks):
+        value = dot(up_full[k], cot[me * own_blocks + k], NT)
+        rank_grad[me * own_blocks + k] = (adapter_scale * value).astype(rank_grad.dtype)
+    grad_copies = [
+        remote(rank_grad.at[chunk(me)], rank_grad.at[chunk(me)], {"tensor": p}) for p in others
+    ]
+    for c in grad_copies:
+        c.start()
+
+    copy_a.wait_recv()
+    copy_c.start()
+    copy_d.start()
+    for c in grad_copies:
+        c.wait_recv()
+
+    term_copies = []
+    for i, p in enumerate((jx, jd, js, job)):
+        for s in range(SLOT_CAP):
+            index, valid = slot(p, s)
+            live = lax.broadcasted_iota(jnp.int32, (1, BLOCK), 1) < (
+                fill_ref[base + index] * valid
+            )
+            rows = jnp.where(live, rank_grad[index].astype(jnp.float32), 0.0).astype(
+                rank_grad.dtype
+            )
+            term_send[i, s] = jnp.dot(
+                rows, tokens[index], preferred_element_type=jnp.float32
+            ).astype(term_send.dtype)
+        if i < 3:
+            c = remote(term_send.at[i], got_terms.at[job], {"job": p})
+            c.start()
+            term_copies.append(c)
+        else:
+            own_terms = load(term_send.at[i], got_terms.at[job])
+        if i == 1:
+            gather_recv(1)
+            if n > 3:
+                gather_send(2)
+            sum_send(1)
+
+    copy_c.wait_recv()
+    copy_e.start()
+    for s in range(2, n - 1):
+        gather_recv(s)
+        if s + 1 < n - 1:
+            gather_send(s + 1)
+        sum_send(s)
+    down_load.wait()
+    copy_b.wait_recv()
+    copy_d.wait_recv()
+    copy_e.wait_recv()
+
+    for b in range(blocks):
+        value = dot(down_all[adapter[b]], tokens[b], NT)
+        rank_part[b // own_blocks, b % own_blocks] = jnp.where(live_row(b), value, 0.0).astype(
+            rank_part.dtype
+        )
+    rank_copies = [remote(rank_part.at[p], rank_in.at[me], {"tensor": p}) for p in others]
+    for c in rank_copies:
+        c.start()
+
+    out_copies = []
+    tile_out = 512
+
+    def token_chunk(z):
+        @pl.loop(0, width // tile_out)
+        def _(t):
+            columns = pl.ds(pl.multiple_of(t * tile_out, tile_out), tile_out)
+            rows = cot[pl.ds(z * own_blocks, own_blocks)].reshape(own_blocks * BLOCK, key_width)
+            acc = dot(rows, weight[columns, :], NT)
+            for k in range(own_blocks):
+                b = z * own_blocks + k
+                value = acc[k * BLOCK : (k + 1) * BLOCK] + dot(
+                    rank_grad[b], down_all[adapter[b], :, columns], TN
+                )
+                staged[b, :, columns] = jnp.where(live_column(b), value, 0.0).astype(staged.dtype)
+
+        out_copies.append(
+            load(
+                staged.at[pl.ds(z * own_blocks, own_blocks)],
+                grad_tokens_out.at[pl.ds(z * own_blocks, own_blocks)],
+            )
+        )
+
+    for z in range(n // 2):
+        token_chunk(z)
+
+    for c in rank_copies:
+        c.wait_recv()
+    rank_in[me] = rank_part[me]
+    rank_sum = jnp.sum(rank_in[...].astype(jnp.float32), axis=0)
+    rank_sum = rank_sum.astype(jnp.bfloat16)
+    for t in range(n):
+        rank_split[t] = rank_sum[:, t * portion : (t + 1) * portion]
+    mine_copies = [remote(rank_split.at[p], rank_mine.at[chunk(me)], {"tensor": p}) for p in others]
+    for c in mine_copies:
+        c.start()
+    for k in range(own_blocks):
+        rank_mine[me * own_blocks + k] = rank_split[me, k]
+
+    for z in range(n // 2, n):
+        token_chunk(z)
+
+    for c in mine_copies:
+        c.wait_recv()
+    up_term_copies = []
+    for i, p in enumerate((jx, jd, js, job)):
+        for s in range(SLOT_CAP):
+            index, valid = slot(p, s)
+            value = jnp.dot(rank_mine[index], cot[index], preferred_element_type=jnp.float32)
+            up_term_send[i, s] = (
+                jnp.where(valid > 0, adapter_scale, 0.0) * value
+            ).astype(up_term_send.dtype)
+        if i < 3:
+            c = remote(up_term_send.at[i], got_up_terms.at[job], {"job": p})
+            c.start()
+            up_term_copies.append(c)
+        else:
+            own_up_terms = load(up_term_send.at[i], got_up_terms.at[job])
+
+    @pl.when(me >= 1)
+    def _():
+        right_sum[n - 2][1].wait_recv()
+
+    @pl.when(me <= n - 2)
+    def _():
+        left_sum[n - 2][1].wait_recv()
+
+    for k in range(own_blocks):
+        value = part[me * own_blocks + k].astype(jnp.float32) + adapter_scale * dot(
+            rank_sum[k], up_own[:, k].reshape(rank, key_width), TN
+        )
+        value = value + jnp.where(me >= 1, from_left[n - 2, k].astype(jnp.float32), 0.0)
+        value = value + jnp.where(me <= n - 2, from_right[n - 2, k].astype(jnp.float32), 0.0)
+        projected_ref[pl.ds(k * BLOCK, BLOCK), :] = value.astype(projected_ref.dtype)
+
+    for c in term_copies + up_term_copies:
+        c.wait_recv()
+    for c in (
+        up_copies
+        + [copy_a, copy_b, copy_c, copy_d, copy_e]
+        + turn_copies
+        + grad_copies
+        + term_copies
+        + rank_copies
+        + mine_copies
+        + up_term_copies
+    ):
+        c.wait_send()
+    for s in range(n - 1):
+
+        @pl.when((me >= s) & (me <= n - 2))
+        def _(s=s):
+            right_gather[s].wait_send()
+
+        @pl.when((me <= n - 1 - s) & (me >= 1))
+        def _(s=s):
+            left_gather[s].wait_send()
+
+        @pl.when((me <= s) & (me <= n - 2))
+        def _(s=s):
+            right_sum[s][1].wait_send()
+
+        @pl.when((n - 1 - me <= s) & (me >= 1))
+        def _(s=s):
+            left_sum[s][1].wait_send()
+
+    own_terms.wait()
+    own_up_terms.wait()
+    for c in out_copies:
+        c.wait()
+
+
+def owner_sum_kernel(blocks, own_ref, owner_ref, local_ref, got_ref, got_up_ref, down_ref, up_ref):
+    own = own_ref[0]
+    first = pl.program_id(0) == 0
+    down_ref[...] = jnp.zeros_like(down_ref)
+
+    @pl.when(first)
+    def _():
+        up_ref[...] = jnp.zeros_like(up_ref)
+
+    for j in range(got_ref.shape[0]):
+        def step(b, count, j=j):
+            hit = owner_ref[j * blocks + b] == own
+            a = local_ref[j * blocks + b]
+
+            @pl.when(hit)
+            def _():
+                down_ref[a] = down_ref[a] + got_ref[j, count].astype(jnp.float32)
+
+            @pl.when(hit & first)
+            def _():
+                up_ref[a] = up_ref[a] + got_up_ref[j, count].astype(jnp.float32)
+
+            return count + jnp.where(hit, 1, 0)
+
+        lax.fori_loop(0, blocks, step, jnp.int32(0))
+
+
+def owner_sum(own, owners, locals_all, got, got_up, adapters, blocks, tile):
+    jobs, slots, rank, width = got.shape
+    portion, key_width = got_up.shape[2:]
+    return pl.pallas_call(
+        functools.partial(owner_sum_kernel, blocks),
+        grid_spec=pltpu.PrefetchScalarGridSpec(
+            num_scalar_prefetch=3,
+            grid=(width // tile,),
+            in_specs=[
+                pl.BlockSpec((jobs, slots, rank, tile), lambda i, *_: (0, 0, 0, i)),
+                pl.BlockSpec((jobs, slots, portion, key_width), lambda i, *_: (0, 0, 0, 0)),
+            ],
+            out_specs=[
+                pl.BlockSpec((adapters, rank, tile), lambda i, *_: (0, 0, i)),
+                pl.BlockSpec((adapters, portion, key_width), lambda i, *_: (0, 0, 0)),
+            ],
+        ),
+        out_shape=[
+            jax.ShapeDtypeStruct((adapters, rank, width), jnp.float32),
+            jax.ShapeDtypeStruct((adapters, portion, key_width), jnp.float32),
+        ],
+        compiler_params=pltpu.CompilerParams(vmem_limit_bytes=VMEM_LIMIT),
+        name="owner_sum",
+    )(own, owners, locals_all, got, got_up)
+
+
+def local(
+    tokens,
+    frozen_key_weight,
+    adapter_down_maps,
+    adapter_up_maps,
+    cotangent,
+    block_owner_job,
+    block_local_adapter,
+    block_live_rows,
+):
+    own_rows, key_width = cotangent.shape
+    n = lax.axis_size("tensor")
+    jobs = lax.axis_size("job")
+    adapters, width, rank = adapter_down_maps.shape
+    portion = adapter_up_maps.shape[1]
+    fits = own_rows % BLOCK == 0 and n >= 3 and n % 2 == 0 and jobs == 4
+    if not (fits and lax.axis_size("groups") == 2 and adapters % 2 == 0 and portion == 16):
+        return general(
+            tokens,
+            frozen_key_weight,
+            adapter_down_maps,
+            adapter_up_maps,
+            cotangent,
+            block_owner_job,
+            block_local_adapter,
+            block_live_rows,
+        )
+    row_total = tokens.shape[0]
+    blocks = row_total // BLOCK
+    own_blocks = own_rows // BLOCK
+    owners = block_owner_job.reshape(-1)
+    bf16 = jnp.bfloat16
+    hbm = pl.BlockSpec(memory_space=pl.ANY)
+    smem = pl.BlockSpec(memory_space=pltpu.SMEM)
+    copies = 3 + 4 * (n - 1) + 5 + 4 * (n - 1) + 6
+    projected, grad_tokens, got_terms, got_up_terms = pl.pallas_call(
+        functools.partial(main_kernel, n),
+        in_specs=[smem, smem, smem, hbm, hbm, hbm, hbm, hbm],
+        out_specs=[pl.BlockSpec(memory_space=pltpu.VMEM), hbm, hbm, hbm],
+        out_shape=[
+            jax.ShapeDtypeStruct((own_rows, key_width), bf16),
+            jax.ShapeDtypeStruct((blocks, BLOCK, width), bf16),
+            jax.ShapeDtypeStruct((jobs, SLOT_CAP, rank, width), bf16),
+            jax.ShapeDtypeStruct((jobs, SLOT_CAP, portion, key_width), bf16),
+        ],
+        scratch_shapes=[
+            pltpu.VMEM((blocks, BLOCK, width), bf16),
+            pltpu.VMEM(frozen_key_weight.shape, bf16),
+            pltpu.VMEM((jobs * adapters, rank, width), bf16),
+            pltpu.VMEM((jobs * adapters, portion, key_width), bf16),
+            pltpu.VMEM((blocks, BLOCK, key_width), bf16),
+            pltpu.VMEM((blocks, BLOCK, key_width), bf16),
+            pltpu.VMEM((n - 1, own_blocks, BLOCK, key_width), bf16),
+            pltpu.VMEM((n - 1, own_blocks, BLOCK, key_width), bf16),
+            pltpu.VMEM((n, own_blocks, portion, key_width), bf16),
+            pltpu.VMEM((n, own_blocks, portion, key_width), bf16),
+            pltpu.VMEM((blocks, rank, BLOCK), bf16),
+            pltpu.VMEM((n, own_blocks, rank, BLOCK), bf16),
+            pltpu.VMEM((n, own_blocks, rank, BLOCK), bf16),
+            pltpu.VMEM((n, own_blocks, portion, BLOCK), bf16),
+            pltpu.VMEM((blocks, portion, BLOCK), bf16),
+            pltpu.VMEM((jobs, SLOT_CAP, rank, width), bf16),
+            pltpu.VMEM((jobs, SLOT_CAP, portion, key_width), bf16),
+            pltpu.VMEM((blocks, BLOCK, width), bf16),
+            pltpu.SemaphoreType.DMA((7 + n,)),
+            pltpu.SemaphoreType.DMA((copies,)),
+            pltpu.SemaphoreType.DMA((copies,)),
+        ],
+        compiler_params=pltpu.CompilerParams(
+            collective_id=0, has_side_effects=True, vmem_limit_bytes=60 * 1024 * 1024
+        ),
+        cost_estimate=pl.CostEstimate(
+            flops=4 * row_total * width * key_width,
+            bytes_accessed=4 * row_total * width,
+            transcendentals=0,
+        ),
+        name="project_and_grads",
+    )(
+        owners,
+        block_local_adapter,
+        block_live_rows,
+        tokens.reshape(blocks, BLOCK, width),
+        frozen_key_weight,
+        jnp.transpose(adapter_down_maps, (0, 2, 1)),
+        adapter_up_maps,
+        cotangent.reshape(own_blocks, BLOCK, key_width),
+    )
+    own = lax.axis_index("job").astype(jnp.int32).reshape(1)
+    grad_down, grad_up = owner_sum(
+        own, owners, block_local_adapter, got_terms, got_up_terms, adapters, blocks, 512
+    )
+    return (
+        projected,
+        grad_tokens.reshape(row_total, width),
+        jnp.transpose(grad_down, (0, 2, 1)),
+        grad_up,
+    )
+
+
 def solution(mesh):
     placed = (
         P(("groups", "job"), "tensor"),

time: 310 us -> 123 us (0.40)
  waiting for transfers between devices: 147 us -> 0 us
  Pallas kernels: 0 us -> 114 us
  matrix products: 64 us -> 0 us
  local copies, waits for them, and re-layouts: 42.9 us -> 8 us
  other arithmetic: 16.5 us -> 0 us
  blocking collectives: 13.9 us -> 0 us
  between operations: 13.9 us -> 0.69 us
  starting transfers between devices: 10.3 us -> 0 us
    pallas_call x0 -> x2, Pallas kernels: none -> 114 us  [the longest x1 107 us: local(): pl.pallas_call(functools.partial(main_kernel, n), in_specs=[smem, smem, s...]
    all_gather x3 -> x0, waiting for transfers between devices: 73.5 us -> none  [the longest x1 63.3 us: local(): grad_full = lax.all_gather(cotangent, 'tensor', axis=0, tiled=True)]
    dot_general x10 -> x0, matrix products: 64 us -> none  [the longest x1 12.6 us: local(): lax.dot_general(grad_full, frozen_key_weight, (((1,), (1,)), ((), ())), p...]
    all_to_all x2 -> x0, waiting for transfers between devices: 49.9 us -> none  [the longest x1 48.3 us: local(): lax.all_to_all(dense_down.astype(jnp.bfloat16), 'job', split_axis=0, conc...]
    reshape x6 -> x0, local copies, waits for them, and re-layouts: 26.9 us -> none  [the longest x1 14.3 us: local(): down_terms = jnp.einsum('bnd,bnr->bdr', row_blocks, rank_grad_blocks, pre...]
    reduce_scatter x2 -> x0, waiting for transfers between devices: 21.9 us -> none  [the longest x1 21.9 us: local(): lax.psum_scatter(rank_terms.astype(jnp.bfloat16), 'tensor', scatter_dimen...]
    all_gather x1 -> x0, blocking collectives: 13.9 us -> none  [local(): lax.all_gather(rank_grad_mine.reshape(row_total, rank_portion), 'tensor',...]
    all_to_all x2 -> x0, starting transfers between devices: 10.1 us -> none  [the longest x1 5.63 us: local(): lax.all_to_all(dense_down.astype(jnp.bfloat16), 'job', split_axis=0, conc...]
  transfers between devices with their start and end apart: 7 -> 0, of which waited for: 6 -> 0; matrix products, arithmetic and copies ran while one was open for 40% -> 0% of each run, Pallas kernels for 0% -> 0%
where the time goes in v2:
time: 123 us
  Pallas kernels  114 us (93%)
  local copies, waits for them, and re-layouts  8 us (7%)
    pallas_call x1, Pallas kernels, local(): pl.pallas_call(functools.partial(main_kernel, n), in_specs=[smem, smem, s...  107 us
    unnamed x12, local copies, waits for them, and re-layouts  8 us
    pallas_call x1, Pallas kernels, owner_sum(): pl.pallas_call(functools.partial(owner_sum_kernel, blocks), grid_spec=plt...  6.94 us

profile of v2, /device:TPU:0, one launch (start us, length us, event | category | flops | bytes accessed | tf_op | source)
XLA Modules:
  0.0 122.7 jit_solution(7660689503461549735)
XLA Ops:
  0.6 0.0 copy-start.2
  0.6 0.0 copy-start.3
  0.7 107.1 %project_and_grads.1 = (bf16[384,1024]{1,0:T(8,128)(2,1)}, bf16[12,128,2048]{2,1,0:T(8,128)(2,1)}, bf16[4,4,64,2048]{3,2,1,0:T(8,128)(2,1)}, bf16[4,4,16,1024]{3,2,1,0:T(8,128)(2,1)}) custom-call(s32[48]{0:T(128)} %bitcast.7, s32[48]{0:T(128)} %local_ref.3, s32[48]{0:T(128)} %fill_ref.1, bf16[12,128,2048]{2,1,0:T(8,128)(2,1)} %bitcast.10, ...), custom_call_target="tpu_custom_call" | custom-call | flops 12884901888 | bytes 12582912 | tf_op jit(solution)/shard_map/project_and_grads/pallas_call | solution.py:662
  107.8 0.0 copy-done.2
  107.8 0.0 copy-done.3
  107.8 0.0 copy-start
  107.8 2.2 %copy-done = bf16[4,4,64,2048]{3,2,1,0:T(8,128)(2,1)S(1)} copy-done((bf16[4,4,64,2048]{3,2,1,0:T(8,128)(2,1)S(1)}, bf16[4,4,64,2048]{3,2,1,0:T(8,128)(2,1)}, u32[]{:S(2)}) %copy-start) | copy-done | bytes 4194328
  110.0 0.0 copy-start.1
  110.0 1.0 copy-done.1
  111.0 0.0 copy-start.4
  111.0 6.9 %owner_sum.1 = (f32[8,64,2048]{2,1,0:T(8,128)}, f32[8,16,1024]{2,1,0:T(8,128)}) custom-call(s32[1]{0:T(128)} %bitcast.5.own_ref, s32[48]{0:T(128)S(1)} %bitcast.8, s32[48]{0:T(128)S(1)} %copy-done.3, bf16[4,4,64,2048]{3,2,1,0:T(8,128)(2,1)S(1)} %copy-done, bf16[4,4,16,1024]{3,2,1,0:T(8,128)(2,1)S(1)} %copy-done.1), custom_call_target="tpu_custom_call" | custom-call | tf_op jit(solution)/shard_map/owner_sum/pallas_call | solution.py:604
  117.9 2.1 %copy.14 = bf16[384,1024]{1,0:T(8,128)(2,1)} copy(bf16[384,1024]{1,0:T(8,128)(2,1)} %get-tuple-element.20) | data formatting | bytes 1572864
  120.0 0.0 copy-done.4
  120.0 2.7 %copy.15 = bf16[1536,2048]{1,0:T(8,128)(2,1)} copy(bf16[1536,2048]{1,0:T(8,128)(2,1)S(1)} %bitcast.9) | data formatting | bytes 12582912
Async XLA Ops:
  0.6 107.1 %copy-start.2 = (s32[48,1]{0,1:T(1,128)S(1)}, s32[48,1]{0,1:T(1,128)}, u32[]{:S(2)}) copy-start(s32[48,1]{0,1:T(1,128)} %param.13) | copy-start | bytes 580
  0.6 107.1 %copy-start.3 = (s32[48]{0:T(128)S(1)}, s32[48]{0:T(128)}, u32[]{:S(2)}) copy-start(s32[48]{0:T(128)} %local_ref.3) | copy-start | bytes 580
  107.8 2.2 %copy-start = (bf16[4,4,64,2048]{3,2,1,0:T(8,128)(2,1)S(1)}, bf16[4,4,64,2048]{3,2,1,0:T(8,128)(2,1)}, u32[]{:S(2)}) copy-start(bf16[4,4,64,2048]{3,2,1,0:T(8,128)(2,1)} %get-tuple-element.12.got_ref) | copy-start | bytes 12582916
  110.0 1.0 copy-start.1
  111.0 9.0 %copy-start.4 = (bf16[12,128,2048]{2,1,0:T(8,128)(2,1)S(1)}, bf16[12,128,2048]{2,1,0:T(8,128)(2,1)}, u32[]{:S(2)}) copy-start(bf16[12,128,2048]{2,1,0:T(8,128)(2,1)} %get-tuple-element.11) | copy-start | bytes 18874372

commit v3 on v2

--- a/solution.py
+++ b/solution.py
@@ -128,7 +128,7 @@
     return (projected, grad_tokens, grad_down, grad_up)
 
 
-def peers_of(own, groups):
+def peers_of(own):
     x, core = own // 2, own % 2
     return (2 * (1 - x) + core, 2 * (1 - x) + 1 - core, 2 * x + 1 - core)
 
@@ -145,8 +145,8 @@
     cot_in,
     projected_ref,
     grad_tokens_out,
-    got_terms,
-    got_up_terms,
+    grad_down_out,
+    grad_up_out,
     tokens,
     weight,
     down_all,
@@ -165,6 +165,9 @@
     term_send,
     up_term_send,
     staged,
+    got_terms,
+    got_up_terms,
+    down_total,
     load_sem,
     send_sem,
     recv_sem,
@@ -181,7 +184,7 @@
     portion = rank // n
     jobs = 4
     half = adapters // 2
-    jx, jd, js = peers_of(job, None)
+    jx, jd, js = peers_of(job)
     counter = [0]
     loads = [0]
 
@@ -228,10 +231,12 @@
     pl.semaphore_wait(barrier, 3 + len(others) + 1)
 
     up_copies = [
-        remote(up_in, up_all.at[pl.ds(job * adapters, adapters)], {"job": p}) for p in (jx, jd, js)
+        remote(up_in, up_all.at[pl.ds(job * adapters, adapters)], {"job": p}) for p in (jx, js)
     ]
     for c in up_copies:
         c.start()
+    jx_maps = up_all.at[pl.ds(jx * adapters, adapters)]
+    up_copies.append(remote(jx_maps, jx_maps, {"job": js}))
 
     def chunk(index):
         return pl.ds(index * own_blocks, own_blocks)
@@ -274,15 +279,23 @@
 
     gather_send(0)
 
-    def region(owner, h):
-        return down_all.at[pl.ds(owner * adapters + h * half, half)]
-
-    copy_a = remote(down_in.at[pl.ds(group * half, half)], region(job, group), {"job": jx})
+    piece = half // 2
+
+    def region(owner, h, i):
+        return down_all.at[pl.ds(owner * adapters + h * half + i * piece, piece)]
+
+    copy_a = [
+        remote(
+            down_in.at[pl.ds(group * half + i * piece, piece)], region(job, group, i), {"job": jx}
+        )
+        for i in range(2)
+    ]
     copy_b = remote(down_in, down_all.at[pl.ds(job * adapters, adapters)], {"job": js})
-    copy_c = remote(region(jx, group), region(jx, group), {"groups": 1 - group})
-    copy_d = remote(region(jx, group), region(jx, group), {"job": js})
-    copy_e = remote(region(jx, 1 - group), region(jx, 1 - group), {"job": js})
-    copy_a.start()
+    mine = [region(jx, group, i) for i in range(2)]
+    other = [region(jx, 1 - group, i) for i in range(2)]
+    copy_c = [remote(r, r, {"groups": 1 - group}) for r in mine]
+    copy_d = [remote(r, r, {"job": js}) for r in mine]
+    copy_e = [remote(r, r, {"job": js}) for r in other]
     copy_b.start()
 
     base = job * blocks
@@ -313,11 +326,12 @@
     tokens_load.wait()
     tile = 256
     per = blocks // 2
-    for h in range(2):
+
+    def base_product(h):
         masks = [live_column(h * per + k) for k in range(per)]
 
         @pl.loop(0, key_width // tile)
-        def _(t, h=h, masks=masks):
+        def _(t):
             columns = pl.ds(pl.multiple_of(t * tile, tile), tile)
             rows = tokens[pl.ds(h * per, per)].reshape(per * BLOCK, width)
             acc = jnp.dot(rows, weight[:, columns], preferred_element_type=jnp.float32)
@@ -326,9 +340,15 @@
                     masks[k], acc[k * BLOCK : (k + 1) * BLOCK], 0.0
                 ).astype(part.dtype)
 
+    base_product(0)
+
     up_load.wait()
-    for c in up_copies:
-        c.wait_recv()
+    up_copies[0].wait_recv()
+    up_copies[2].start()
+    for c in copy_a:
+        c.start()
+    up_copies[1].wait_recv()
+    up_copies[2].wait_recv()
     turn_copies = [
         remote(up_turn.at[p], up_own.at[me], {"tensor": p}) for p in others
     ]
@@ -337,6 +357,7 @@
     for c in turn_copies:
         c.start()
     up_own[me] = up_turn[me]
+    base_product(1)
 
     cot_load.wait()
     gather_recv(0)
@@ -407,9 +428,12 @@
     for c in grad_copies:
         c.start()
 
-    copy_a.wait_recv()
-    copy_c.start()
-    copy_d.start()
+    def pass_on(i):
+        copy_a[i].wait_recv()
+        copy_c[i].start()
+        copy_d[i].start()
+
+    pass_on(0)
     for c in grad_copies:
         c.wait_recv()
 
@@ -427,28 +451,23 @@
                 rows, tokens[index], preferred_element_type=jnp.float32
             ).astype(term_send.dtype)
         if i < 3:
-            c = remote(term_send.at[i], got_terms.at[job], {"job": p})
+            c = remote(term_send.at[i], got_terms.at[i], {"job": p})
             c.start()
             term_copies.append(c)
-        else:
-            own_terms = load(term_send.at[i], got_terms.at[job])
         if i == 1:
-            gather_recv(1)
-            if n > 3:
-                gather_send(2)
-            sum_send(1)
-
-    copy_c.wait_recv()
-    copy_e.start()
-    for s in range(2, n - 1):
-        gather_recv(s)
-        if s + 1 < n - 1:
-            gather_send(s + 1)
-        sum_send(s)
+            pass_on(1)
+            copy_c[0].wait_recv()
+            copy_e[0].start()
+
+    gather_recv(1)
+    gather_send(2)
+    sum_send(1)
+    copy_c[1].wait_recv()
+    copy_e[1].start()
     down_load.wait()
     copy_b.wait_recv()
-    copy_d.wait_recv()
-    copy_e.wait_recv()
+    for c in copy_d + copy_e:
+        c.wait_recv()
 
     for b in range(blocks):
         value = dot(down_all[adapter[b]], tokens[b], NT)
@@ -459,6 +478,41 @@
     for c in rank_copies:
         c.start()
 
+    def weights_of(p):
+        count = jnp.int32(0)
+        index = [jnp.int32(-1)] * SLOT_CAP
+        for b in range(blocks):
+            hit = jnp.where(owner_ref[p * blocks + b] == job, 1, 0)
+            for k in range(SLOT_CAP):
+                here = hit * jnp.where(count == k, 1, 0)
+                index[k] = index[k] + here * (local_ref[p * blocks + b] + 1)
+            count = count + hit
+        return [
+            [jnp.where(index[k] == a, 1.0, 0.0) for k in range(SLOT_CAP)] for a in range(adapters)
+        ]
+
+    lanes = 128
+
+    def take_terms(got, p, first):
+        weights = weights_of(p)
+
+        @pl.loop(0, width // lanes)
+        def _(t):
+            columns = pl.ds(pl.multiple_of(t * lanes, lanes), lanes)
+            values = [got[k, :, columns].astype(jnp.float32) for k in range(SLOT_CAP)]
+            for a in range(adapters):
+                total = None if first else down_total[a, :, columns]
+                for k in range(SLOT_CAP):
+                    term = weights[a][k] * values[k]
+                    total = term if total is None else total + term
+                down_total[a, :, columns] = total
+
+    take_terms(term_send.at[3], job, True)
+    term_copies[2].wait_recv()
+    take_terms(got_terms.at[2], js, False)
+
+    gather_recv(2)
+    sum_send(2)
     out_copies = []
     tile_out = 512
 
@@ -512,11 +566,12 @@
                 jnp.where(valid > 0, adapter_scale, 0.0) * value
             ).astype(up_term_send.dtype)
         if i < 3:
-            c = remote(up_term_send.at[i], got_up_terms.at[job], {"job": p})
+            c = remote(up_term_send.at[i], got_up_terms.at[i], {"job": p})
             c.start()
             up_term_copies.append(c)
-        else:
-            own_up_terms = load(up_term_send.at[i], got_up_terms.at[job])
+
+    term_copies[0].wait_recv()
+    take_terms(got_terms.at[0], jx, False)
 
     @pl.when(me >= 1)
     def _():
@@ -534,11 +589,27 @@
         value = value + jnp.where(me <= n - 2, from_right[n - 2, k].astype(jnp.float32), 0.0)
         projected_ref[pl.ds(k * BLOCK, BLOCK), :] = value.astype(projected_ref.dtype)
 
-    for c in term_copies + up_term_copies:
+    term_copies[1].wait_recv()
+    take_terms(got_terms.at[1], jd, False)
+    down_out = load(down_total, grad_down_out)
+    for c in up_term_copies:
         c.wait_recv()
+    sources = [(got_up_terms.at[i], p) for i, p in enumerate((jx, jd, js))]
+    sources.append((up_term_send.at[3], job))
+    tables = [weights_of(p) for _, p in sources]
+    for a in range(adapters):
+        total = jnp.zeros((portion, key_width), jnp.float32)
+        for (got, _), table in zip(sources, tables):
+            for k in range(SLOT_CAP):
+                total = total + table[a][k] * got[k].astype(jnp.float32)
+        grad_up_out[a] = total
     for c in (
         up_copies
-        + [copy_a, copy_b, copy_c, copy_d, copy_e]
+        + copy_a
+        + [copy_b]
+        + copy_c
+        + copy_d
+        + copy_e
         + turn_copies
         + grad_copies
         + term_copies
@@ -565,63 +636,9 @@
         def _(s=s):
             left_sum[s][1].wait_send()
 
-    own_terms.wait()
-    own_up_terms.wait()
+    down_out.wait()
     for c in out_copies:
         c.wait()
-
-
-def owner_sum_kernel(blocks, own_ref, owner_ref, local_ref, got_ref, got_up_ref, down_ref, up_ref):
-    own = own_ref[0]
-    first = pl.program_id(0) == 0
-    down_ref[...] = jnp.zeros_like(down_ref)
-
-    @pl.when(first)
-    def _():
-        up_ref[...] = jnp.zeros_like(up_ref)
-
-    for j in range(got_ref.shape[0]):
-        def step(b, count, j=j):
-            hit = owner_ref[j * blocks + b] == own
-            a = local_ref[j * blocks + b]
-
-            @pl.when(hit)
-            def _():
-                down_ref[a] = down_ref[a] + got_ref[j, count].astype(jnp.float32)
-
-            @pl.when(hit & first)
-            def _():
-                up_ref[a] = up_ref[a] + got_up_ref[j, count].astype(jnp.float32)
-
-            return count + jnp.where(hit, 1, 0)
-
-        lax.fori_loop(0, blocks, step, jnp.int32(0))
-
-
-def owner_sum(own, owners, locals_all, got, got_up, adapters, blocks, tile):
-    jobs, slots, rank, width = got.shape
-    portion, key_width = got_up.shape[2:]
-    return pl.pallas_call(
-        functools.partial(owner_sum_kernel, blocks),
-        grid_spec=pltpu.PrefetchScalarGridSpec(
-            num_scalar_prefetch=3,
-            grid=(width // tile,),
-            in_specs=[
-                pl.BlockSpec((jobs, slots, rank, tile), lambda i, *_: (0, 0, 0, i)),
-                pl.BlockSpec((jobs, slots, portion, key_width), lambda i, *_: (0, 0, 0, 0)),
-            ],
-            out_specs=[
-                pl.BlockSpec((adapters, rank, tile), lambda i, *_: (0, 0, i)),
-                pl.BlockSpec((adapters, portion, key_width), lambda i, *_: (0, 0, 0)),
-            ],
-        ),
-        out_shape=[
-            jax.ShapeDtypeStruct((adapters, rank, width), jnp.float32),
-            jax.ShapeDtypeStruct((adapters, portion, key_width), jnp.float32),
-        ],
-        compiler_params=pltpu.CompilerParams(vmem_limit_bytes=VMEM_LIMIT),
-        name="owner_sum",
-    )(own, owners, locals_all, got, got_up)
 
 
 def local(
@@ -639,8 +656,8 @@
     jobs = lax.axis_size("job")
     adapters, width, rank = adapter_down_maps.shape
     portion = adapter_up_maps.shape[1]
-    fits = own_rows % BLOCK == 0 and n >= 3 and n % 2 == 0 and jobs == 4
-    if not (fits and lax.axis_size("groups") == 2 and adapters % 2 == 0 and portion == 16):
+    fits = own_rows % BLOCK == 0 and n == 4 and jobs == 4
+    if not (fits and lax.axis_size("groups") == 2 and adapters % 4 == 0 and portion == 16):
         return general(
             tokens,
             frozen_key_weight,
@@ -656,18 +673,19 @@
     own_blocks = own_rows // BLOCK
     owners = block_owner_job.reshape(-1)
     bf16 = jnp.bfloat16
+    vmem = pl.BlockSpec(memory_space=pltpu.VMEM)
     hbm = pl.BlockSpec(memory_space=pl.ANY)
     smem = pl.BlockSpec(memory_space=pltpu.SMEM)
-    copies = 3 + 4 * (n - 1) + 5 + 4 * (n - 1) + 6
-    projected, grad_tokens, got_terms, got_up_terms = pl.pallas_call(
+    copies = 8 * (n - 1) + 18
+    projected, grad_tokens, grad_down, grad_up = pl.pallas_call(
         functools.partial(main_kernel, n),
         in_specs=[smem, smem, smem, hbm, hbm, hbm, hbm, hbm],
-        out_specs=[pl.BlockSpec(memory_space=pltpu.VMEM), hbm, hbm, hbm],
+        out_specs=[vmem, hbm, hbm, vmem],
         out_shape=[
             jax.ShapeDtypeStruct((own_rows, key_width), bf16),
             jax.ShapeDtypeStruct((blocks, BLOCK, width), bf16),
-            jax.ShapeDtypeStruct((jobs, SLOT_CAP, rank, width), bf16),
-            jax.ShapeDtypeStruct((jobs, SLOT_CAP, portion, key_width), bf16),
+            jax.ShapeDtypeStruct((adapters, rank, width), jnp.float32),
+            jax.ShapeDtypeStruct((adapters, portion, key_width), jnp.float32),
         ],
         scratch_shapes=[
             pltpu.VMEM((blocks, BLOCK, width), bf16),
@@ -688,7 +706,10 @@
             pltpu.VMEM((jobs, SLOT_CAP, rank, width), bf16),
             pltpu.VMEM((jobs, SLOT_CAP, portion, key_width), bf16),
             pltpu.VMEM((blocks, BLOCK, width), bf16),
-            pltpu.SemaphoreType.DMA((7 + n,)),
+            pltpu.VMEM((jobs - 1, SLOT_CAP, rank, width), bf16),
+            pltpu.VMEM((jobs - 1, SLOT_CAP, portion, key_width), bf16),
+            pltpu.VMEM((adapters, rank, width), jnp.float32),
+            pltpu.SemaphoreType.DMA((6 + n,)),
             pltpu.SemaphoreType.DMA((copies,)),
             pltpu.SemaphoreType.DMA((copies,)),
         ],
@@ -711,10 +732,6 @@
         adapter_up_maps,
         cotangent.reshape(own_blocks, BLOCK, key_width),
     )
-    own = lax.axis_index("job").astype(jnp.int32).reshape(1)
-    grad_down, grad_up = owner_sum(
-        own, owners, block_local_adapter, got_terms, got_up_terms, adapters, blocks, 512
-    )
     return (
         projected,
         grad_tokens.reshape(row_total, width),

time: 123 us -> 119 us (0.967)
  Pallas kernels: 114 us -> 106 us
  local copies, waits for them, and re-layouts: 8 us -> 11.6 us
    pallas_call x1 -> x0, Pallas kernels: 6.94 us -> none  [owner_sum(): pl.pallas_call(functools.partial(owner_sum_kernel, blocks), grid_spec=plt...]
    unnamed x12 -> x8, local copies, waits for them, and re-layouts: 8 us -> 11.6 us
    pallas_call x1, Pallas kernels: 107 us -> 106 us  [local(): pl.pallas_call(functools.partial(main_kernel, n), in_specs=[smem, smem, s...]
where the time goes in v3:
time: 119 us; the launch traced here: 118 us
  Pallas kernels  106 us (89%)
  local copies, waits for them, and re-layouts  11.6 us (10%)
    pallas_call x1, Pallas kernels, local(): pl.pallas_call(functools.partial(main_kernel, n), in_specs=[smem, smem, s...  106 us
    unnamed x8, local copies, waits for them, and re-layouts  11.6 us

profile of v3, /device:TPU:0, one launch (start us, length us, event | category | flops | bytes accessed | tf_op | source)
XLA Modules:
  0.0 118.1 jit_solution(1444694777625864342)
XLA Ops:
  0.6 105.8 %project_and_grads.1 = (bf16[384,1024]{1,0:T(8,128)(2,1)}, bf16[12,128,2048]{2,1,0:T(8,128)(2,1)}, f32[8,64,2048]{2,1,0:T(8,128)}, f32[8,16,1024]{2,1,0:T(8,128)}) custom-call(s32[48]{0:T(128)} %bitcast.11, s32[48]{0:T(128)} %local_ref.1, s32[48]{0:T(128)} %fill_ref.1, bf16[12,128,2048]{2,1,0:T(8,128)(2,1)} %bitcast.8, bf16[2048,1024]{1,0:T(8,128)(2,1)} %weight_in.1, ...), custom_call_target="tpu_custom_call" | custom-call | flops 12884901888 | bytes 12582912 | tf_op jit(solution)/shard_map/project_and_grads/pallas_call | solution.py:680
  106.4 2.1 %copy.16 = bf16[384,1024]{1,0:T(8,128)(2,1)} copy(bf16[384,1024]{1,0:T(8,128)(2,1)} %get-tuple-element.16) | data formatting | bytes 1572864
  108.5 0.0 copy-start
  108.5 6.8 %copy.17 = bf16[1536,2048]{1,0:T(8,128)(2,1)} copy(bf16[1536,2048]{1,0:T(8,128)(2,1)} %bitcast.6) | data formatting | bytes 12582912
  115.3 0.0 copy-done
  115.3 0.0 copy-start.1
  115.3 2.0 %copy.18 = f32[8,2048,64]{1,2,0:T(8,128)} copy(f32[8,2048,64]{1,2,0:T(8,128)S(1)} %bitcast.7) | data formatting | bytes 8388608
  117.3 0.0 copy-done.1
  117.3 0.8 copy.19
Async XLA Ops:
  108.5 6.8 %copy-start = (f32[8,64,2048]{2,1,0:T(8,128)S(1)}, f32[8,64,2048]{2,1,0:T(8,128)}, u32[]{:S(2)}) copy-start(f32[8,64,2048]{2,1,0:T(8,128)} %get-tuple-element.10) | copy-start | bytes 12582916
  115.3 2.0 %copy-start.1 = (f32[8,16,1024]{2,1,0:T(8,128)S(1)}, f32[8,16,1024]{2,1,0:T(8,128)}, u32[]{:S(2)}) copy-start(f32[8,16,1024]{2,1,0:T(8,128)} %get-tuple-element.19) | copy-start | bytes 1572868
